TPU v7x, 128 devices: a whole 4x4x4 slice. The times are simulated.
128 devices in a mesh: batch: 4 (over y_lo, core), seq: 16 (over z, x), tensor: 2 (over y_hi).
Axes of the slice: x: 4, y: 4 (y_hi: 2, y_lo: 2; y = y_hi * 2 + y_lo), z: 4, core: 2. Of those that a mesh axis runs over, the one named last changes fastest.
Arguments:
- latents: bfloat16 [64, 512, 1024], P(('batch', 'seq'), 'tensor'), may hold values from -6 to 6
- pixels: bfloat16 [64, 4096, 261], P('batch', ('seq', 'tensor')), may hold values from -6 to 6
- crop_bounds: int32 [64, 2], P(('batch', 'seq')), may hold values from 0 to 4096, as said below
- key_mask: int32 [64, 4096], P(('batch', 'seq')), may hold values 0 or 1
- query_gain: bfloat16 [1024], replicated, may hold values from 0.25 to 1.75
- pixel_gain: bfloat16 [261], replicated, may hold values from 0.25 to 1.75
- cross_gain: bfloat16 [1024], replicated, may hold values from 0.25 to 1.75
- attend_gain: bfloat16 [1024], replicated, may hold values from 0.25 to 1.75
- feed_gain: bfloat16 [1024], replicated, may hold values from 0.25 to 1.75
- query_weight: bfloat16 [1024, 1024], replicated, may hold values from -0.1875 to 0.1875
- key_weight: bfloat16 [261, 1024], replicated, may hold values from -0.375 to 0.375
- value_weight: bfloat16 [261, 1024], replicated, may hold values from -0.375 to 0.375
- cross_out: bfloat16 [1024, 1024], replicated, may hold values from -6 to 6
- cross_up: bfloat16 [1024, 1024], replicated, may hold values from -0.1875 to 0.1875
- cross_down: bfloat16 [1024, 1024], replicated, may hold values from -0.1875 to 0.1875
- self_attend: bfloat16 [3, 1024, 1024], P(None, None, 'tensor'), may hold values from -0.1875 to 0.1875
- self_out: bfloat16 [1024, 1024], P('tensor'), may hold values from -2.5 to 2.5
- self_up: bfloat16 [1024, 1024], P(None, 'tensor'), may hold values from -0.1875 to 0.1875
- self_down: bfloat16 [1024, 1024], P('tensor'), may hold values from -0.1875 to 0.1875
- cotangent: bfloat16 [64, 512, 1024], P(('batch', 'seq'), 'tensor'), may hold values from -6 to 6
Outputs:
- latents_out: bfloat16 [64, 512, 1024], P(('batch', 'seq'), 'tensor')
- latents_grad: float32 [64, 512, 1024], P(('batch', 'seq'), 'tensor')
- pixels_grad: float32 [64, 4096, 261], P('batch', ('seq', 'tensor'))
- querygain_grad: float32 [1024], P(('seq', 'tensor'))
- pixelgain_grad: float32 [261], replicated
- crossgain_grad: float32 [1024], P(('seq', 'tensor'))
- attendgain_grad: float32 [1024], P(('seq', 'tensor'))
- feedgain_grad: float32 [1024], P(('seq', 'tensor'))
- queryweight_grad: float32 [1024, 1024], P(('seq', 'tensor'))
- keyweight_grad: float32 [261, 1024], P(None, ('seq', 'tensor'))
- valueweight_grad: float32 [261, 1024], P(None, ('seq', 'tensor'))
- crossout_grad: float32 [1024, 1024], P(('seq', 'tensor'))
- crossup_grad: float32 [1024, 1024], P(('seq', 'tensor'))
- crossdown_grad: float32 [1024, 1024], P(('seq', 'tensor'))
- selfattend_grad: float32 [3, 1024, 1024], P(None, 'seq', 'tensor')
- selfout_grad: float32 [1024, 1024], P('tensor', 'seq')
- selfup_grad: float32 [1024, 1024], P('seq', 'tensor')
- selfdown_grad: float32 [1024, 1024], P('tensor', 'seq')
Inputs may be any that keep to these rules, and one draw needn't show every extreme that they name: crop_bounds[i] = (start, count): image i's crop keeps pixel rows start to start + count - 1; count >= 2048 and start + count <= 4096.
All inputs are finite; a program needn't handle non-finite values. No bound on the sum of `key_mask` on one device may be relied on, other than what follows from the above.
Results may differ from a plain program's by a relative error of at most 0.033.
Values may be sent and summed in bfloat16 or wider, within the bound.
A program may use at most 192 MiB of HBM per device.

v0:
```python
import functools
import math

import jax
import jax.numpy as jnp
from jax import lax
from jax.experimental import pallas as pl
from jax.experimental.pallas import tpu as pltpu
from jax.sharding import PartitionSpec as P

HEAD_WIDTH = 128
EPS = 1e-05
MASKED = -1000000000.0
MESH = pl.DeviceIdType.MESH
F32 = jnp.float32
B16 = jnp.bfloat16
LANES = 128
PAD = 272
WIDE = 1024
CYCLE = ("XA", "XB", "ZA", "ZB", "T")

def norm_parts(values):
    average = jnp.mean(values, axis=-1, keepdims=True)
    centered = values - average
    spread = jnp.mean(centered * centered, axis=-1, keepdims=True)
    inverse = lax.rsqrt(spread + EPS)
    return centered * inverse, inverse


def dot(a, b):
    return jnp.dot(a, b, preferred_element_type=F32)


def dot_t(a, b):
    return lax.dot_general(a, b, (((1,), (1,)), ((), ())), preferred_element_type=F32)


def tdot(a, b):
    return lax.dot_general(a, b, (((0,), (0,)), ((), ())), preferred_element_type=F32)


def flip(p):
    return p + 1 - 2 * lax.rem(p, 2)


def place():
    b, s, t = lax.axis_index("batch"), lax.axis_index("seq"), lax.axis_index("tensor")
    return lax.div(b, 2), lax.rem(b, 2), s, t


MIB = 1024 * 1024
ROWS = 256
GELU_K = math.sqrt(2.0 / math.pi)


def gelu(u):
    return 0.5 * u * (1.0 + jnp.tanh(GELU_K * (u + 0.044715 * u * u * u)))


def gelu_slope(u):
    th = jnp.tanh(GELU_K * (u + 0.044715 * u * u * u))
    return 0.5 * (1.0 + th) + 0.5 * u * (1.0 - th * th) * GELU_K * (1.0 + 3.0 * 0.044715 * u * u)


def loop(n, step):
    lax.fori_loop(0, n, lambda i, carry: (step(i), carry)[1], 0)


def block(i, n):
    return pl.ds(pl.multiple_of(i * n, n), n)


FRONT_HBM = (
    ("home", "kept", "latents", "cotangent", "self_attend", "self_out", "self_up", "self_down")
    + ("query_weight", "key_wide", "value_wide", "cross_out", "cross_up", "cross_down")
)
FRONT_VMEM = ("query_gain", "cross_gain", "attend_gain", "feed_gain")
FRONT_OUT = {
    "cot": ((ROWS, WIDE), B16),
    "feed_in": ((ROWS, WIDE), B16),
    "feed_act": ((ROWS, WIDE), B16),
    "feed_back": ((ROWS, WIDE), B16),
    "branch": ((512, WIDE), B16),
    "mixed": ((512, 512), B16),
    "attend_in": ((512, WIDE), B16),
    "back": ((512, 1536), B16),
    "cross_act": ((ROWS, WIDE), B16),
    "cross_in": ((ROWS, WIDE), B16),
    "attended": ((ROWS, WIDE), B16),
    "late_x": ((ROWS, WIDE), B16),
    "late_x_give": ((ROWS, WIDE), B16),
    "mixed_pixels": ((ROWS, 512), B16),
    "mixed_pixels_give": ((ROWS, 512), B16),
    "rows_grad": ((ROWS, WIDE), F32),
    "rows_grad_give": ((ROWS, WIDE), B16),
    "after_mlp": ((ROWS, WIDE), F32),
    "attend_grad": ((ROWS, WIDE), F32),
    "cross_hidden": ((ROWS, WIDE), F32),
    "after_cross": ((ROWS, WIDE), F32),
    "latents_turned": ((ROWS, WIDE), B16),
    "picture": ((PAD, 4096), B16),
    "raised": ((ROWS, 4096), B16),
    "mixed_f32": ((ROWS, PAD), F32),
    "asked": ((ROWS, PAD), B16),
    "latents_out": ((ROWS, WIDE), B16),
    "inverse_total": ((ROWS, 1), F32),
    "any_kept": ((1, 1), F32),
    "feedgain": ((1, WIDE), F32),
}
FRONT_OUT_VMEM = ("inverse_total", "any_kept", "feedgain")


def front_kernel(names, sems, *refs):
    l, c, s, t = place()
    seq = 16
    r = dict(zip(names, refs))
    send, recv, local = r["send"], r["recv"], r["local"]
    cross_scale = 1.0 / math.sqrt(WIDE)
    self_scale = 1.0 / math.sqrt(HEAD_WIDTH)
    sib = (2 * l + 1 - c, s, t)
    over = (2 * (1 - l) + c, s, 1 - t)
    beside = (2 * (1 - l) + c, s, t)

    def peer(k):
        return (2 * l + t, lax.rem(s + k, seq), c)

    barrier = pltpu.get_barrier_semaphore()
    for device in (sib, over, beside):
        pl.semaphore_signal(barrier, inc=1, device_id=device, device_id_type=MESH)
    for k in range(1, seq):
        pl.semaphore_signal(barrier, inc=1, device_id=peer(k), device_id_type=MESH)

    @pl.when(c != t)
    def _():
        pl.semaphore_signal(barrier, inc=1, device_id=peer(0), device_id_type=MESH)
        pl.semaphore_wait(barrier, 3 + seq)

    @pl.when(c == t)
    def _():
        pl.semaphore_wait(barrier, 2 + seq)

    used = [0, 0]
    waits, stores = [], []

    def remote_of(src, dst, device):
        i = used[0]
        used[0] += 1
        return pltpu.make_async_remote_copy(
            src_ref=src, dst_ref=dst, send_sem=send.at[i], recv_sem=recv.at[i], device_id=device, device_id_type=MESH
        )

    def remote(src, dst, device):
        copy = remote_of(src, dst, device)
        copy.start()
        waits.append(copy)
        return copy

    def here_of(src, dst):
        i = used[1]
        used[1] += 1
        return pltpu.make_async_copy(src, dst, local.at[i])

    def here(src, dst):
        copy = here_of(src, dst)
        copy.start()
        return copy

    def store(name, src):
        stores.append(here(src, r[name]))

    ready = {}

    def await_all(*wanted):
        for name in wanted:
            for wait in ready.pop(name, ()):
                wait()

    base = pl.multiple_of(c * (seq * LANES), LANES)
    far = pl.multiple_of(t * (seq * LANES), LANES)
    picture = r["v_picture"]

    def away_of(k):
        return remote_of(
            r["home"].at[lax.rem(s + k, seq)],
            picture.at[:, pl.ds(pl.multiple_of(far + s * LANES, LANES), LANES)],
            peer(k),
        )

    away = [away_of(k) for k in range(seq)]
    lat_move, cot_move = remote_of(r["latents"], r["v_lat"], peer(0)), remote_of(r["cotangent"], r["v_cot"], peer(0))
    kept_move = remote_of(r["kept"], r["v_kept"], sib)
    lat_stay, cot_stay = here_of(r["latents"], r["v_lat"]), here_of(r["cotangent"], r["v_cot"])
    kept_stay = here_of(r["kept"], r["v_kept"])
    picture_stay = here_of(r["home"].at[s], picture.at[:, pl.ds(pl.multiple_of(base + s * LANES, LANES), LANES)])

    @pl.when(c != t)
    def _():
        lat_move.start()
        away[0].start()

    @pl.when(c == t)
    def _():
        lat_stay.start()
        picture_stay.start()
        kept_stay.start()
        kept_move.start()
        cot_stay.start()

    for k in range(1, seq):
        away[k].start()

    mine, theirs = l, 1 - l

    def rows128(base_row, p):
        return pl.ds(pl.multiple_of(base_row + 128 * p, 128), 128)

    own256 = 256 * c
    own_columns = pl.ds(pl.multiple_of(own256, LANES), 256)
    attend_far, out_w, up_w, down_w = r["w_attend_far"], r["w_out"], r["w_up"], r["w_down"]

    def attend_piece(k, p):
        return attend_far.at[k, block(p, 512)]

    across = {}
    for k in range(3):
        across["attend%d" % k] = remote(
            r["self_attend"].at[k, block(theirs, 512), own_columns], attend_piece(k, theirs), over
        )

    @pl.when(c != t)
    def _():
        cot_move.start()

    across["out"] = remote(r["self_out"].at[rows128(own256, theirs)], out_w.at[rows128(256, theirs)], over)
    across["up"] = remote(
        r["self_up"].at[:, rows128(own256, theirs)], up_w.at[:, rows128(512, theirs)], over
    )
    across["down"] = remote(r["self_down"].at[rows128(own256, theirs)], down_w.at[rows128(512, theirs)], over)

    for name, to in (
        ("query_weight", "w_query"),
        ("key_wide", "w_key"),
        ("value_wide", "w_value"),
        ("cross_out", "w_cross_out"),
        ("cross_up", "w_cross_up"),
        ("cross_down", "w_cross_down"),
    ):
        ready[to] = [here(r[name], r[to]).wait]
    ready["attend_own"] = [here(r["self_attend"].at[:, :, own_columns], r["w_attend_own"]).wait]
    ready["out_own"] = [
        here(r["self_out"].at[pl.ds(pl.multiple_of(own256, LANES), 256)], out_w.at[pl.ds(0, 256)]).wait,
        here(r["self_out"].at[pl.ds(pl.multiple_of(256 - own256, LANES), 256)], out_w.at[pl.ds(512, 256)]).wait,
    ]
    ready["up_own"] = [here(r["self_up"], up_w.at[:, pl.ds(0, 512)]).wait]
    ready["down_own"] = [here(r["self_down"], down_w.at[pl.ds(0, 512)]).wait]

    places = {
        "attend0": lambda p: attend_piece(0, p),
        "attend1": lambda p: attend_piece(1, p),
        "attend2": lambda p: attend_piece(2, p),
        "out": lambda p: out_w.at[rows128(256, p)],
        "up": lambda p: up_w.at[:, rows128(512, p)],
        "down": lambda p: down_w.at[rows128(512, p)],
    }
    sib_places = {
        "out": lambda p: out_w.at[rows128(768, p)],
        "up": lambda p: up_w.at[:, rows128(768, p)],
        "down": lambda p: down_w.at[rows128(768, p)],
    }
    onward = {}

    def pass_on(*wanted):
        for name in wanted:
            across[name].wait_recv()
            at = places[name]
            onward[name] = [remote(at(mine), at(mine), beside)]
            if name in sib_places:
                to = sib_places[name]
                onward[name].append(remote(at(mine), to(mine), sib))

    def pass_rest(*wanted):
        for name in wanted:
            onward[name][0].wait_recv()
            if name in sib_places:
                at, to = places[name], sib_places[name]
                onward[name].append(remote(at(theirs), to(theirs), sib))

    def arrived(*wanted):
        for name in wanted:
            for copy in onward[name][1:]:
                copy.wait_recv()

    def norm_rows(value_ref, gain, out_ref, also=None):
        def step(i):
            rows = block(i, 64)
            v = value_ref[rows, :].astype(F32)
            high, _ = norm_parts(v)
            out_ref[rows, :] = (high * gain).astype(B16)

        loop(ROWS // 64, step)

    def each256(n, step):
        loop(n // 256, lambda i: step(block(i, 256)))

    @pl.when(c != t)
    def _():
        lat_move.wait_recv()

    @pl.when(c == t)
    def _():
        lat_stay.wait()

    store("latents_turned", r["v_lat"])
    query_low, queries = r["v_query_low"], r["v_queries"]
    norm_rows(r["v_lat"], r["query_gain"][...], query_low)
    await_all("w_query", "w_key")

    def query_step(columns):
        queries[:, columns] = dot(query_low[...], r["w_query"][:, columns]).astype(B16)

    each256(WIDE, query_step)
    r["v_asked"][...] = (dot_t(queries[...], r["w_key"][...]) * cross_scale).astype(B16)
    store("asked", r["v_asked"])
    late_a, late_b = here_of(query_low, r["late_x"]), here_of(queries, r["late_x_give"])
    late_c, late_d = here_of(query_low, r["late_x_give"]), here_of(queries, r["late_x"])

    @pl.when(c == 0)
    def _():
        late_a.start()
        late_b.start()

    @pl.when(c == 1)
    def _():
        late_c.start()
        late_d.start()

    def chunk(k):
        return picture.at[:, pl.ds(pl.multiple_of(base + lax.rem(s - k + seq, seq) * LANES, LANES), LANES)]

    @pl.when(c != t)
    def _():
        away[0].wait_recv()
        kept_move.wait_recv()

    @pl.when(c == t)
    def _():
        picture_stay.wait()
        kept_stay.wait()

    passed = [remote(chunk(0), chunk(0), sib)]
    for k in range(1, seq):
        away[k].wait_recv()
        passed.append(remote(chunk(k), chunk(k), sib))
    for copy in passed:
        copy.wait_recv()
    store("picture", picture)

    scores, raised = r["v_scores"], r["v_raised"]
    r["v_top"][...] = jnp.full((ROWS, 1), -3.0e38, F32)
    r["v_total"][...] = jnp.zeros((ROWS, 1), F32)
    r["v_mixed"][...] = jnp.zeros_like(r["v_mixed"])
    r["any_kept"][...] = jnp.max(r["v_kept"][0:1, :], axis=-1, keepdims=True)

    def score_step(i):
        columns = block(i, 512)
        value = dot(r["v_asked"][...], picture[:, columns])
        value = jnp.where(r["v_kept"][0:1, columns] > 0.5, value, MASKED)
        scores[:, columns] = value
        r["v_top"][...] = jnp.maximum(r["v_top"][...], jnp.max(value, axis=-1, keepdims=True))

    loop(8, score_step)

    def raise_step(i):
        columns = block(i, 512)
        value = jnp.exp(scores[:, columns] - r["v_top"][...])
        r["v_total"][...] += jnp.sum(value, axis=-1, keepdims=True)
        low = value.astype(B16)
        raised[:, columns] = low
        r["v_mixed"][...] += dot_t(low, picture[:, columns])

    loop(8, raise_step)
    store("raised", raised)
    inverse_total = 1.0 / r["v_total"][...]
    r["inverse_total"][...] = inverse_total
    mixed = r["v_mixed"][...] * inverse_total
    r["v_mixed"][...] = mixed
    store("mixed_f32", r["v_mixed"])
    r["v_mixed_wide"][...] = jnp.zeros_like(r["v_mixed_wide"])
    r["v_mixed_wide"][:, :PAD] = mixed
    tail = pltpu.roll(r["v_mixed_wide"][:, 256:384], 16, 1).astype(B16)
    for name, core in (("mixed_pixels", c), ("mixed_pixels_give", 1 - c)):
        ref = r["v_" + name]
        ref[:, :256] = jnp.zeros((ROWS, 256), B16)
        ref[:, 256:384] = tail
        ref[:, 384:] = r["v_mixed_wide"][:, pl.ds(pl.multiple_of(LANES * core, LANES), LANES)].astype(B16)
        store(name, ref)
    await_all("w_value", "w_cross_out")
    r["v_attended"][...] = dot(mixed.astype(B16), r["w_value"][...]).astype(B16)
    store("attended", r["v_attended"])

    def out_step(columns):
        r["v_after_cross"][:, columns] = r["v_lat"][:, columns].astype(F32) + dot(
            r["v_attended"][...], r["w_cross_out"][:, columns]
        )

    each256(WIDE, out_step)
    store("after_cross", r["v_after_cross"])
    pass_on("attend0")
    norm_rows(r["v_after_cross"], r["cross_gain"][...], r["v_cross_in"])
    store("cross_in", r["v_cross_in"])
    await_all("w_cross_up", "w_cross_down")

    def up_step(columns):
        hidden = dot(r["v_cross_in"][...], r["w_cross_up"][:, columns])
        r["v_hidden"][:, columns] = hidden
        r["v_cross_act"][:, columns] = gelu(hidden).astype(B16)

    each256(WIDE, up_step)
    store("cross_hidden", r["v_hidden"])
    store("cross_act", r["v_cross_act"])
    pass_on("attend1")

    def down_step(columns):
        r["v_after_mlp"][:, columns] = r["v_after_cross"][:, columns] + dot(
            r["v_cross_act"][...], r["w_cross_down"][:, columns]
        )

    each256(WIDE, down_step)
    store("after_mlp", r["v_after_mlp"])

    attend_in = r["v_attend_in"]
    top, low = pl.ds(0, ROWS), pl.ds(ROWS, ROWS)
    norm_rows(r["v_after_mlp"], r["attend_gain"][...], attend_in)
    attend_copy = remote(attend_in.at[top], attend_in.at[low], sib)
    await_all("attend_own")
    pass_on("attend2")
    attend_copy.wait_recv()
    store("attend_in", attend_in)
    projected, probs = r["v_projected"], r["v_probs"]

    def project(weights, at):
        for k in range(3):
            projected[k, :, pl.ds(at, 256)] = dot(attend_in[...], weights[k]).astype(B16)

    def attend(h):
        columns = block(h, HEAD_WIDTH)
        dotted = dot_t(projected[0, :, columns], projected[1, :, columns]) * self_scale
        value = jnp.exp(dotted - jnp.max(dotted, axis=-1, keepdims=True))
        value = (value * (1.0 / jnp.sum(value, axis=-1, keepdims=True))).astype(B16)
        probs[h] = value
        r["v_self"][:, columns] = dot(value, projected[2, :, columns]).astype(B16)

    project(r["w_attend_own"], 0)
    loop(2, attend)
    pass_rest("attend0", "attend1", "attend2")
    project(attend_far, 256)
    loop(2, lambda i: attend(i + 2))
    store("mixed", r["v_self"])
    self_copy = remote(r["v_self"].at[low], r["v_self_in"], sib)
    pass_on("out", "up")
    await_all("out_own")
    pass_rest("out")
    arrived("out")
    self_copy.wait_recv()

    def attended_step(columns):
        r["v_after_attend"][:, columns] = (
            r["v_after_mlp"][:, columns]
            + dot(r["v_self"][top, :], out_w[pl.ds(0, 512), columns])
            + dot(r["v_self_in"][...], out_w[pl.ds(512, 512), columns])
        )

    each256(WIDE, attended_step)

    norm_rows(r["v_after_attend"], r["feed_gain"][...], r["v_feed_in"])
    store("feed_in", r["v_feed_in"])

    @pl.when(c != t)
    def _():
        cot_move.wait_recv()

    @pl.when(c == t)
    def _():
        cot_stay.wait()

    store("cot", r["v_cot"])
    pass_on("down")
    await_all("up_own", "down_own")

    def feed_step(columns):
        hidden = dot(r["v_feed_in"][...], up_w[:, columns])
        r["v_feed_act"][:, columns] = gelu(hidden).astype(B16)
        pulled = dot_t(r["v_cot"][...], down_w[columns, :])
        r["v_feed_back"][:, columns] = (gelu_slope(hidden) * pulled).astype(B16)

    loop(2, lambda i: feed_step(block(i, 256)))
    pass_rest("up", "down")
    arrived("up", "down")
    loop(2, lambda i: feed_step(block(i + 2, 256)))
    store("feed_act", r["v_feed_act"])
    store("feed_back", r["v_feed_back"])

    def feed_pull(rows):
        r["v_tmp"][:, rows] = dot_t(r["v_feed_back"][...], up_w[rows, :])

    each256(WIDE, feed_pull)
    r["feedgain"][...] = jnp.zeros((1, WIDE), F32)
    branch = r["v_branch"]

    def feed_norm(i):
        rows = block(i, 64)
        high, inverse = norm_parts(r["v_after_attend"][rows, :])
        e = r["v_tmp"][rows, :]
        a = e * r["feed_gain"][...]
        back = (
            a - jnp.mean(a, axis=-1, keepdims=True) - high * jnp.mean(a * high, axis=-1, keepdims=True)
        ) * inverse
        r["feedgain"][...] += jnp.sum(e * high, axis=0, keepdims=True)
        total = r["v_cot"][rows, :].astype(F32) + back
        r["v_attend_grad"][rows, :] = total
        branch[rows, :] = total.astype(B16)

    loop(ROWS // 64, feed_norm)
    branch_copy = remote(branch.at[top], branch.at[low], sib)
    store("attend_grad", r["v_attend_grad"])

    def latents_step(columns):
        r["v_latents_out"][:, columns] = (
            r["v_after_attend"][:, columns] + dot(r["v_feed_act"][...], down_w[:, columns])
        ).astype(B16)

    each256(WIDE, latents_step)
    store("latents_out", r["v_latents_out"])
    branch_copy.wait_recv()
    store("branch", branch)

    def mixed_step(rows):
        r["v_self_grad"][:, rows] = dot_t(branch[...], out_w[rows, :]).astype(B16)

    loop(2, lambda i: mixed_step(block(i, 256)))
    back = r["v_back"]

    def attend_back(h):
        columns = block(h, HEAD_WIDTH)
        grad = r["v_self_grad"][:, columns]
        p = probs[h]
        g = dot_t(grad, projected[2, :, columns])
        p32 = p.astype(F32)
        change = (p32 * (g - jnp.sum(p32 * g, axis=-1, keepdims=True))).astype(B16)
        back[:, pl.ds(pl.multiple_of(h * HEAD_WIDTH, LANES), HEAD_WIDTH)] = (
            dot(change, projected[1, :, columns]) * self_scale
        ).astype(B16)
        back[:, pl.ds(pl.multiple_of(512 + h * HEAD_WIDTH, LANES), HEAD_WIDTH)] = (
            tdot(change, projected[0, :, columns]) * self_scale
        ).astype(B16)
        back[:, pl.ds(pl.multiple_of(1024 + h * HEAD_WIDTH, LANES), HEAD_WIDTH)] = tdot(p, grad).astype(B16)

    loop(4, attend_back)
    store("back", back)

    def rows_step(rows):
        total = 0
        for k in range(3):
            total = total + dot_t(back[:, pl.ds(512 * k, 256)], r["w_attend_own"][k, rows, :])
            total = total + dot_t(back[:, pl.ds(512 * k + 256, 256)], attend_far[k, rows, :])
        r["v_tmp"][:, rows] = total[:ROWS]
        r["v_rows_give"][:, rows] = total[ROWS:].astype(B16)

    each256(WIDE, rows_step)
    store("rows_grad", r["v_tmp"])
    store("rows_grad_give", r["v_rows_give"])

    @pl.when(c != t)
    def _():
        lat_move.wait_send()
        cot_move.wait_send()
        away[0].wait_send()

    @pl.when(c == t)
    def _():
        kept_move.wait_send()

    @pl.when(c == 0)
    def _():
        late_a.wait()
        late_b.wait()

    @pl.when(c == 1)
    def _():
        late_c.wait()
        late_d.wait()

    for k in range(1, seq):
        away[k].wait_send()
    for copy in waits:
        copy.wait_send()
    for copy in stores:
        copy.wait()
    assert not ready, tuple(ready)
    assert used[0] <= sems[0] and used[1] <= sems[1], used


def front(given):
    names, scratch = [], []

    def room(name, shape, dtype=B16):
        names.append(name)
        scratch.append(pltpu.VMEM(shape, dtype))

    sems = (64, 64)
    names += list(FRONT_HBM) + list(FRONT_VMEM) + list(FRONT_OUT)
    for name in ("send", "recv", "local"):
        names.append(name)
        scratch.append(pltpu.SemaphoreType.DMA((sems[1 if name == "local" else 0],)))
    for name in ("query", "cross_out", "cross_up", "cross_down", "out", "up", "down"):
        room("w_" + name, (WIDE, WIDE))
    for name in ("key", "value"):
        room("w_" + name, (PAD, WIDE))
    for name in ("attend_own", "attend_far"):
        room("w_" + name, (3, WIDE, 256))
    room("v_picture", (PAD, 4096))
    room("v_kept", (8, 4096), F32)
    room("v_scores", (ROWS, 4096), F32)
    room("v_raised", (ROWS, 4096))
    for name in ("lat", "cot", "query_low", "queries", "attended", "cross_in", "cross_act", "feed_in", "feed_act"):
        room("v_" + name, (ROWS, WIDE))
    for name in ("feed_back", "latents_out", "rows_give"):
        room("v_" + name, (ROWS, WIDE))
    for name in ("after_cross", "hidden", "after_mlp", "after_attend", "attend_grad", "tmp"):
        room("v_" + name, (ROWS, WIDE), F32)
    for name in ("attend_in", "branch"):
        room("v_" + name, (512, WIDE))
    room("v_projected", (3, 512, 512))
    room("v_probs", (4, 512, 512))
    room("v_self", (512, 512))
    room("v_self_in", (ROWS, 512))
    room("v_self_grad", (512, 512))
    room("v_back", (512, 1536))
    room("v_asked", (ROWS, PAD))
    room("v_top", (ROWS, 1), F32)
    room("v_total", (ROWS, 1), F32)
    room("v_mixed", (ROWS, PAD), F32)
    room("v_mixed_wide", (ROWS, 384), F32)
    room("v_mixed_pixels", (ROWS, 512))
    room("v_mixed_pixels_give", (ROWS, 512))
    anywhere = pl.BlockSpec(memory_space=pl.ANY)
    vmem = pl.BlockSpec(memory_space=pltpu.VMEM)
    result = pl.pallas_call(
        functools.partial(front_kernel, tuple(names), sems),
        out_shape=[jax.ShapeDtypeStruct(*spec) for spec in FRONT_OUT.values()],
        in_specs=[anywhere] * len(FRONT_HBM) + [vmem] * len(FRONT_VMEM),
        out_specs=[vmem if name in FRONT_OUT_VMEM else anywhere for name in FRONT_OUT],
        scratch_shapes=scratch,
        compiler_params=pltpu.CompilerParams(collective_id=0, has_side_effects=True, vmem_limit_bytes=63 * MIB),
        name="front",
    )(*[given[name] for name in FRONT_HBM + FRONT_VMEM])
    return dict(zip(FRONT_OUT, result))


SETS = ("S", "P", "Q")
WIDTHS = {"S": 384, "P": 256, "Q": 256}
DEPTHS = {"S": 64, "P": 32, "Q": 32}
PART_ORDERS = (
    ("XA", "ZA", "XB", "ZB"),
    ("ZA", "XB", "ZB", "XA"),
    ("XB", "ZB", "XA", "ZA"),
    ("ZB", "XA", "ZA", "XB"),
)
X_NAMES = ("cot", "feed_in", "branch", "attend_in", "cross_act", "cross_in", "attended", "late_x")
Y_NAMES = ("feed_act", "feed_back", "mixed", "back", "mixed_pixels")
HBM_INPUTS = (
    ("cot", "feed_in", "feed_act", "feed_back", "branch", "mixed", "attend_in", "back")
    + ("cross_act", "cross_in", "attended", "late_x", "late_x_give", "mixed_pixels", "mixed_pixels_give")
    + ("rows_grad", "rows_grad_give", "after_mlp", "attend_grad", "cross_hidden", "after_cross", "latents")
    + ("cross_down", "cross_up", "cross_out", "query_weight", "key_wide", "value_wide", "picture", "raised")
    + ("mixed_f32", "asked", "latents_out")
)
VMEM_INPUTS = ("inverse_total", "any_kept", "attend_gain", "cross_gain", "query_gain", "pixel_gain", "feedgain")


def back_kernel(names, sems, *refs):
    l, c, s, t = place()
    z, x = lax.div(s, 4), lax.rem(s, 4)
    seq = 16
    r = dict(zip(names, refs))
    send, recv, local = r["send"], r["recv"], r["local"]
    cross_scale = 1.0 / math.sqrt(WIDE)

    partner = {
        "XA": (2 * l + c, z * 4 + flip(x), t),
        "XB": (2 * l + c, z * 4 + 3 - x, t),
        "ZA": (2 * l + c, flip(z) * 4 + x, t),
        "ZB": (2 * l + c, (3 - z) * 4 + x, t),
        "T": (2 * l + c, s, 1 - t),
        "L": (2 * (1 - l) + c, s, t),
        "C": (2 * l + 1 - c, s, t),
    }

    def peer(k):
        return (2 * l + t, lax.rem(s + k, seq), c)

    barrier = pltpu.get_barrier_semaphore()
    for device in partner.values():
        pl.semaphore_signal(barrier, inc=1, device_id=device, device_id_type=MESH)
    for k in range(1, seq):
        pl.semaphore_signal(barrier, inc=1, device_id=peer(k), device_id_type=MESH)

    @pl.when(c != t)
    def _():
        pl.semaphore_signal(barrier, inc=1, device_id=peer(0), device_id_type=MESH)
        pl.semaphore_wait(barrier, len(partner) + seq)

    @pl.when(c == t)
    def _():
        pl.semaphore_wait(barrier, len(partner) + seq - 1)

    used = [0, 0]
    waits = []

    def remote_of(src, dst, device):
        i = used[0]
        used[0] += 1
        return pltpu.make_async_remote_copy(
            src_ref=src, dst_ref=dst, send_sem=send.at[i], recv_sem=recv.at[i], device_id=device, device_id_type=MESH
        )

    def remote(src, dst, device):
        copy = remote_of(src, dst, device)
        copy.start()
        waits.append(copy)
        return copy

    def here_of(src, dst):
        i = used[1]
        used[1] += 1
        return pltpu.make_async_copy(src, dst, local.at[i])

    def here(src, dst):
        copy = here_of(src, dst)
        copy.start()
        return copy

    ready = {}

    def await_all(*wanted):
        for name in wanted:
            for wait in ready.pop(name, ()):
                wait()

    sib = partner["C"]
    top, low = pl.ds(0, ROWS), pl.ds(ROWS, ROWS)
    keep512 = pl.ds(pl.multiple_of(512 * c, LANES), 512)
    give512 = pl.ds(pl.multiple_of(512 * (1 - c), LANES), 512)
    keep256 = pl.ds(pl.multiple_of(256 * c, LANES), 256)
    give256 = pl.ds(pl.multiple_of(256 * (1 - c), LANES), 256)
    left, right = pl.ds(0, 256), pl.ds(256, 256)

    def exchange_rows(name, give=None):
        ref, to = r[name], r["x_" + name]
        give = ref if give is None else r[give]
        ready["x_" + name] = [here(ref, to.at[top]).wait, remote(give, to.at[low], sib).wait_recv]

    def exchange_quarter(name):
        ref, to = r[name], r["y_" + name]
        ready["y_" + name] = [
            here(ref.at[:, keep256], to.at[top, left]).wait,
            here(ref.at[:, pl.ds(512, 256)], to.at[top, right]).wait,
            remote(ref.at[:, give256], to.at[low, left], sib).wait_recv,
            remote(ref.at[:, pl.ds(768, 256)], to.at[low, right], sib).wait_recv,
        ]

    def load(name, to, key=None):
        ready[key or name] = [here(r[name], to).wait]

    ready["rows_grad_sum"] = [remote(r["rows_grad_give"], r["v_rows_in"], sib).wait_recv]
    exchange_rows("cot")
    exchange_quarter("feed_act")
    exchange_rows("feed_in")
    exchange_quarter("feed_back")
    load("branch", r["x_branch"], "x_branch")
    load("mixed", r["y_mixed"], "y_mixed")
    load("attend_in", r["x_attend_in"], "x_attend_in")
    load("back", r["y_back"], "y_back")
    load("rows_grad", r["v_tmp"], "rows_grad")
    load("after_mlp", r["v_norm"], "after_mlp")
    load("attend_grad", r["v_grad"], "attend_grad")
    load("cross_down", r["w_down"], "w_down")
    load("cross_up", r["w_up"], "w_up")
    load("cross_hidden", r["v_hidden"], "cross_hidden")
    exchange_rows("cross_act")
    exchange_rows("cross_in")
    load("value_wide", r["w_value"], "w_value")
    load("picture", r["v_picture"], "picture")
    load("raised", r["v_raised"], "raised")
    load("mixed_f32", r["v_mixed"], "mixed_f32")
    load("asked", r["v_asked"], "asked")
    exchange_rows("attended")
    exchange_rows("late_x", "late_x_give")
    ready["y_mixed_pixels"] = [
        here(r["mixed_pixels"], r["y_mixed_pixels"].at[top]).wait,
        remote(r["mixed_pixels_give"], r["y_mixed_pixels"].at[low], sib).wait_recv,
    ]
    load("key_wide", r["w_key"], "w_key")
    load("latents", r["v_latents"], "latents")

    turned = [("latents_out", "latents_home"), ("v_latgrad", "latgrad_home")]
    moves = [remote_of(r[src], r[dst], peer(0)) for src, dst in turned]
    stays = [here_of(r[src], r[dst]) for src, dst in turned]

    class Part:
        def __init__(self, set_, q):
            self.set, self.q, self.stage, self.n, self.cur = set_, q, -1, seq, r["%s%d_buf" % (set_, q)]
            self.weight = {bit: 8 >> k for k, bit in enumerate(PART_ORDERS[q])}

        def index(self, za, zb, xa, xb):
            w = self.weight
            return za * w["ZA"] + zb * w["ZB"] + xa * w["XA"] + xb * w["XB"]

        def begin(self):
            self.stage += 1
            k, n, key = self.stage, self.n, "%s%d_" % (self.set, self.q)
            if k < 4:
                self.into = r[key + "in%d" % k]
                self.copy = remote(self.cur.at[:, pl.ds(n // 2, n // 2)], self.into, partner[PART_ORDERS[self.q][k]])
            elif k == 4:
                self.into = r[key + "in4"]
                self.copy = remote(self.cur.at[1 - t, 0], self.into, partner["T"])
            elif k == 5:
                self.into = r[key + "in5"]
                self.copy = remote(r[key + "sum4"], self.into, partner["L"])
            else:
                width = WIDTHS[self.set]
                dst = r["out_" + self.set].at[:, pl.ds(pl.multiple_of((4 * c + self.q) * width, LANES), width)]
                self.copy = remote(r[key + "sum5"], dst, partner["C"])
                self.copy_here = here(r[key + "sum5"], dst)

        def finish(self):
            self.copy.wait_recv()
            k, key = self.stage, "%s%d_" % (self.set, self.q)
            if k < 4:
                self.n //= 2
                cur, into = self.cur, self.into
                for h in range(2):

                    def step(i, h=h):
                        cur[h, i] = (cur[h, i].astype(F32) + into[h, i].astype(F32)).astype(B16)

                    if self.n > 1:
                        loop(self.n, step)
                    else:
                        step(0)
            elif k == 4:
                r[key + "sum4"][...] = (self.cur[t, 0].astype(F32) + self.into[...].astype(F32)).astype(B16)
            elif k == 5:
                r[key + "sum5"][...] = (r[key + "sum4"][...].astype(F32) + self.into[...].astype(F32)).astype(B16)
            else:
                self.copy_here.wait()

        def advance(self):
            self.finish()
            if self.stage < 6:
                self.begin()

    parts = {(set_, q): Part(set_, q) for set_ in SETS for q in range(4)}

    def advance(set_):
        for q in range(4):
            parts[set_, q].advance()

    def product(x_ref, y_ref, width, set_, pieces, add=False):
        block = 512 if width <= 512 else 256
        per = block // 256

        def step(i):
            columns = pl.ds(pl.multiple_of(i * block, block), block)
            whole = tdot(x_ref[:, columns], y_ref[...])
            for a in range(per):
                zz = i * per + a
                zb = lax.rem(lax.div(z, 2) + lax.div(zz, 2), 2)
                za = lax.rem(lax.rem(z, 2) + lax.rem(zz, 2) + zb, 2)
                for xx in range(4):
                    xb = lax.rem(lax.div(x, 2) + xx // 2, 2)
                    xa = lax.rem(lax.rem(x, 2) + xx % 2 + xb, 2)
                    at = (a * 4 + xx) * 64
                    for src, half, dst, n in pieces:
                        part = parts[set_, dst // WIDTHS[set_]]
                        to = pl.ds(dst % WIDTHS[set_], n)
                        idx = part.index(za, zb, xa, xb)
                        value = whole[at : at + 64, src : src + n]
                        if half is not None:
                            part.cur[half, idx, :, to] = value.astype(B16)
                        else:
                            for h in range(2):
                                piece = value[32 * h : 32 * h + 32]
                                if add:
                                    piece = piece + part.cur[h, idx, :, to].astype(F32)
                                part.cur[h, idx, :, to] = piece.astype(B16)

        loop(WIDE // block, step)

    def spread_pieces(src, half, dst, n, width):
        found = []
        while n > 0:
            m = min(n, width - dst % width)
            found.append((src, half, dst, m))
            src, dst, n = src + m, dst + m, n - m
        return found

    def heads(src, dst):
        return spread_pieces(src, t, dst, 256, 384) + spread_pieces(src + 256, 1 - t, dst, 256, 384)

    def rows_of(src, dst, n):
        return spread_pieces(src, None, dst, n, 256)

    await_all("x_cot", "y_feed_act")
    product(r["x_cot"], r["y_feed_act"], 512, "S", heads(0, 0))
    await_all("x_feed_in", "y_feed_back")
    product(r["x_feed_in"], r["y_feed_back"], 512, "S", heads(0, 256))
    parts["S", 0].begin()
    await_all("x_branch", "y_mixed")
    product(r["x_branch"], r["y_mixed"], 512, "S", heads(0, 512))
    parts["S", 1].begin()
    await_all("x_attend_in", "y_back")
    product(r["x_attend_in"], r["y_back"], 1536, "S", [p for k in range(3) for p in heads(512 * k, 768 + 256 * k)])
    parts["S", 2].begin()
    parts["S", 3].begin()

    out_w, query_w = r["x_cot"], r["x_branch"]
    out_w2, query_w2 = r["x_feed_in"], r["x_attend_in"]
    ready["w_out"] = [
        here(r["cross_out"].at[pl.ds(0, 512)], out_w).wait,
        here(r["cross_out"].at[pl.ds(512, 512)], out_w2).wait,
    ]
    ready["w_query"] = [
        here(r["query_weight"].at[pl.ds(0, 512)], query_w).wait,
        here(r["query_weight"].at[pl.ds(512, 512)], query_w2).wait,
    ]

    def norm_grad(value_ref, gain, slot, after):
        r["gains"][pl.ds(slot, 1), :] = jnp.zeros((1, WIDE), F32)

        def step(i):
            rows = pl.ds(pl.multiple_of(i * 64, 64), 64)
            v = value_ref[rows, :].astype(F32)
            high, inverse = norm_parts(v)
            e = r["v_tmp"][rows, :]
            a = e * gain
            back = (
                a - jnp.mean(a, axis=-1, keepdims=True) - high * jnp.mean(a * high, axis=-1, keepdims=True)
            ) * inverse
            r["gains"][pl.ds(slot, 1), :] += jnp.sum(e * high, axis=0, keepdims=True)
            total = r["v_grad"][rows, :] + back
            after(rows, total)

        loop(ROWS // 64, step)

    def keep_grad(low_ref):
        def after(rows, total):
            r["v_grad"][rows, :] = total
            low_ref[rows, :] = total.astype(B16)

        return after

    def pull(a_ref, pieces, store):
        at = 0
        for piece in pieces:
            n = piece.shape[0]

            def step(i, piece=piece, at=at):
                rows = pl.ds(pl.multiple_of(i * 256, 256), 256)
                store(pl.ds(pl.multiple_of(at + i * 256, 256), 256), dot_t(a_ref[...], piece[rows, :]))

            loop(n // 256, step)
            at += n

    def to_tmp(columns, value):
        r["v_tmp"][:, columns] = value

    r["gains"][...] = jnp.zeros_like(r["gains"])
    await_all("rows_grad", "rows_grad_sum", "after_mlp", "attend_grad")

    def sum_step(i):
        rows = pl.ds(pl.multiple_of(i * 64, 64), 64)
        r["v_tmp"][rows, :] += r["v_rows_in"][rows, :].astype(F32)

    loop(ROWS // 64, sum_step)
    norm_grad(r["v_norm"], r["attend_gain"][...], 2, keep_grad(r["v_branch"]))
    load("after_cross", r["v_norm"], "after_cross")
    ready["y_mlp"] = [
        here(r["v_branch"].at[:, keep512], r["y_mlp"].at[top]).wait,
        remote(r["v_branch"].at[:, give512], r["y_mlp"].at[low], sib).wait_recv,
    ]
    await_all("w_down", "cross_hidden")

    def hidden_store(columns, value):
        r["v_back"][:, columns] = (gelu_slope(r["v_hidden"][:, columns]) * value).astype(B16)

    pull(r["v_branch"], [r["w_down"]], hidden_store)
    ready["y_hidden"] = [
        here(r["v_back"].at[:, keep512], r["y_hidden"].at[top]).wait,
        remote(r["v_back"].at[:, give512], r["y_hidden"].at[low], sib).wait_recv,
    ]
    await_all("w_up")
    pull(r["v_back"], [r["w_up"]], to_tmp)
    await_all("after_cross")
    norm_grad(r["v_norm"], r["cross_gain"][...], 1, keep_grad(r["v_branch2"]))
    ready["y_out"] = [
        here(r["v_branch2"].at[:, keep512], r["y_out"].at[top]).wait,
        remote(r["v_branch2"].at[:, give512], r["y_out"].at[low], sib).wait_recv,
    ]
    await_all("x_cross_act", "y_mlp")
    product(r["x_cross_act"], r["y_mlp"], 512, "P", rows_of(0, 0, 512))
    parts["P", 0].begin()
    parts["P", 1].begin()
    await_all("x_cross_in", "y_hidden")
    product(r["x_cross_in"], r["y_hidden"], 512, "P", rows_of(0, 512, 512))
    parts["P", 2].begin()
    parts["P", 3].begin()
    advance("S")

    await_all("w_out")
    attended_grad = r["x_attended_grad"]

    def attended_store(columns, value):
        attended_grad[top, columns] = value.astype(B16)

    pull(r["v_branch2"], [out_w, out_w2], attended_store)
    ready["x_attended_grad"] = [remote(attended_grad.at[top], attended_grad.at[low], sib).wait_recv]
    await_all("w_value", "mixed_f32", "asked", "picture", "raised")
    mixed_pull = dot_t(attended_grad[top, :], r["w_value"][...])
    pull_low = mixed_pull.astype(B16)
    r["v_pull"][...] = pull_low
    pull_f32 = pull_low.astype(F32)
    r["v_dot"][...] = jnp.sum(pull_f32 * r["v_mixed"][...], axis=-1, keepdims=True)
    scale_any = r["inverse_total"][...] * r["any_kept"][...]
    r["v_asked_t"][...] = (r["v_asked"][...].astype(F32) * scale_any).T.astype(B16)
    r["v_pull_t"][...] = (pull_f32 * r["inverse_total"][...]).T.astype(B16)
    r["v_sum"][...] = jnp.zeros_like(r["v_sum"])
    half = seq * LANES

    def pixel_chunk(start, to, at):
        columns = pl.ds(start, 512)
        picture, raised = r["v_picture"][:, columns], r["v_raised"][:, columns]
        change = (raised.astype(F32) * (dot(r["v_pull"][...], picture) - r["v_dot"][...])).astype(B16)
        r["v_sum"][...] += dot_t(change, picture)
        to[:, pl.ds(at, 512)] = (dot(r["v_asked_t"][...], change) + dot(r["v_pull_t"][...], raised)).astype(B16)

    def far_step(i):
        pixel_chunk(pl.multiple_of((1 - c) * half + i * 512, 512), r["grad_far"], pl.multiple_of(i * 512, 512))

    def near_step(i):
        pixel_chunk(pl.multiple_of(c * half + i * 512, 512), r["grad_own"], pl.multiple_of(i * 512, 512))

    loop(4, far_step)
    grad_copy = remote(r["grad_far"], r["grad_in"], sib)
    advance("S")
    advance("P")
    loop(4, near_step)

    turned_sum = r["v_sum"][...] * scale_any
    r["y_late"][...] = jnp.zeros_like(r["y_late"])
    r["y_late_own"][...] = jnp.zeros_like(r["y_late_own"])
    r["y_late_own"][:, :PAD] = (turned_sum * cross_scale).astype(B16)
    ready["y_late"] = [
        here(r["y_late_own"], r["y_late"].at[top]).wait,
        remote(r["y_late_own"], r["y_late_in"], sib).wait_recv,
    ]
    r["gains"][4:5, :PAD] = (
        jnp.sum(r["v_asked"][...].astype(F32) * turned_sum + r["v_pull"][...].astype(F32) * r["v_mixed"][...], axis=0, keepdims=True)
        / r["pixel_gain"][...]
    )

    grad_copy.wait_recv()

    def grad_step(i):
        rows = pl.ds(pl.multiple_of(i * 16, 16), 16)
        r["grad_own"][rows, :] = (r["grad_own"][rows, :].astype(F32) + r["grad_in"][rows, :].astype(F32)).astype(B16)

    loop(PAD // 16, grad_step)
    first, last_local = used[0], used[1]
    used[0] += seq
    used[1] += 1

    def homeward(k):
        to = lax.rem(s + k, seq)
        return pltpu.make_async_remote_copy(
            src_ref=r["grad_own"].at[:, pl.ds(pl.multiple_of(to * LANES, LANES), LANES)],
            dst_ref=r["home"].at[s],
            send_sem=send.at[first + k],
            recv_sem=recv.at[first + k],
            device_id=peer(k),
            device_id_type=MESH,
        )

    stay = pltpu.make_async_copy(
        r["grad_own"].at[:, pl.ds(pl.multiple_of(s * LANES, LANES), LANES)], r["home"].at[s], local.at[last_local]
    )

    @pl.when(c != t)
    def _():
        homeward(0).start()

    @pl.when(c == t)
    def _():
        stay.start()

    for k in range(1, seq):
        homeward(k).start()

    await_all("x_attended", "y_out")
    product(r["x_attended"], r["y_out"], 512, "Q", rows_of(0, 0, 512))
    parts["Q", 0].begin()
    parts["Q", 1].begin()
    await_all("x_attended_grad", "y_mixed_pixels")
    product(r["x_attended_grad"], r["y_mixed_pixels"], 512, "Q", rows_of(0, 512, 512))
    await_all("x_late_x", "y_late")
    r["y_late"][low, :] = r["y_late_in"][...]
    product(r["x_late_x"], r["y_late"], 384, "Q", rows_of(0, 512, 384), add=True)
    parts["Q", 2].begin()
    parts["Q", 3].begin()
    advance("S")
    advance("P")

    await_all("w_key", "w_query", "latents")
    r["v_rows_in"][...] = dot(r["y_late_own"][:, :PAD], r["w_key"][...]).astype(B16)
    pull(r["v_rows_in"], [query_w, query_w2], to_tmp)

    def latents_after(rows, total):
        r["v_latgrad"][rows, :] = total.astype(B16)

    norm_grad(r["v_latents"], r["query_gain"][...], 0, latents_after)
    r["gains"][3:4, :] = r["feedgain"][...]

    @pl.when(c != t)
    def _():
        for copy in moves:
            copy.start()

    @pl.when(c == t)
    def _():
        for copy in stays:
            copy.start()

    gain_buf, gain_in = r["gain_buf"], r["gain_in"]
    gain_buf[0] = r["gains"][...]
    gain_steps = ("XA", "XB", "ZA", "ZB", "T", "L", "C")
    gain_copy = remote(gain_buf.at[0], gain_in.at[0], partner[gain_steps[0]])
    live = [parts[set_, q] for set_ in SETS for q in range(4)]
    k = 0
    while live or k < 7:
        if k < 7:
            gain_copy.wait_recv()
            total = gain_buf[k] + gain_in[k]
            k += 1
            if k < 7:
                gain_buf[k] = total
                gain_copy = remote(gain_buf.at[k], gain_in.at[k], partner[gain_steps[k]])
            else:
                r["out_gains"][...] = total
        left_over = []
        for part in live:
            last = part.stage == 6
            part.advance()
            if not last:
                left_over.append(part)
        live = left_over

    @pl.when(c != t)
    def _():
        for copy in moves:
            copy.wait()
        homeward(0).wait()

    @pl.when(c == t)
    def _():
        for copy in stays:
            copy.wait()
        stay.wait()

    for k in range(1, seq):
        homeward(k).wait()
    for copy in waits:
        copy.wait_send()
    assert not ready, tuple(ready)
    assert used[0] <= sems[0] and used[1] <= sems[1], used


def back_and_reduce(given):
    names, scratch = [], []

    def room(name, shape, dtype=B16):
        names.append(name)
        scratch.append(pltpu.VMEM(shape, dtype))

    outs = {
        "out_S": ((64, 8 * 384), B16),
        "out_P": ((32, 8 * 256), B16),
        "out_Q": ((32, 8 * 256), B16),
        "home": ((16, PAD, LANES), B16),
        "latents_home": ((ROWS, WIDE), B16),
        "latgrad_home": ((ROWS, WIDE), B16),
        "out_gains": ((8, WIDE), F32),
    }
    sems = (160, 96)
    names += list(HBM_INPUTS) + list(VMEM_INPUTS) + list(outs)
    for name in ("send", "recv", "local"):
        names.append(name)
        scratch.append(pltpu.SemaphoreType.DMA((sems[1 if name == "local" else 0],)))
    for name in X_NAMES + ("attended_grad",):
        room("x_" + name, (512, WIDE))
    for name in ("feed_act", "feed_back", "mixed", "mixed_pixels", "mlp", "hidden", "out"):
        room("y_" + name, (512, 512))
    room("y_back", (512, 1536))
    room("y_late", (512, 384))
    room("y_late_own", (ROWS, 384))
    room("y_late_in", (ROWS, 384))
    for name in ("w_down", "w_up"):
        room(name, (WIDE, WIDE))
    for name in ("w_key", "w_value"):
        room(name, (PAD, WIDE))
    for name in ("v_tmp", "v_norm", "v_grad", "v_hidden"):
        room(name, (ROWS, WIDE), F32)
    for name in ("v_rows_in", "v_branch", "v_branch2", "v_back", "v_latents", "v_latgrad"):
        room(name, (ROWS, WIDE))
    room("v_picture", (PAD, 4096))
    room("v_raised", (ROWS, 4096))
    room("v_mixed", (ROWS, PAD), F32)
    room("v_sum", (ROWS, PAD), F32)
    room("v_asked", (ROWS, PAD))
    room("v_pull", (ROWS, PAD))
    room("v_asked_t", (PAD, ROWS))
    room("v_pull_t", (PAD, ROWS))
    room("v_dot", (ROWS, 1), F32)
    for name in ("grad_own", "grad_far", "grad_in"):
        room(name, (PAD, 16 * LANES))
    room("gains", (8, WIDE), F32)
    room("gain_buf", (7, 8, WIDE), F32)
    room("gain_in", (7, 8, WIDE), F32)
    for set_ in SETS:
        for q in range(4):
            key, depth, width = "%s%d_" % (set_, q), DEPTHS[set_], WIDTHS[set_]
            room(key + "buf", (2, 16, depth, width))
            for k in range(4):
                room(key + "in%d" % k, (2, 8 >> k, depth, width))
            for name in ("in4", "in5", "sum4", "sum5"):
                room(key + name, (depth, width))
    anywhere = pl.BlockSpec(memory_space=pl.ANY)
    vmem = pl.BlockSpec(memory_space=pltpu.VMEM)
    result = pl.pallas_call(
        functools.partial(back_kernel, tuple(names), sems),
        out_shape=[jax.ShapeDtypeStruct(*spec) for spec in outs.values()],
        in_specs=[anywhere] * len(HBM_INPUTS) + [vmem] * len(VMEM_INPUTS),
        out_specs=[anywhere] * (len(outs) - 1) + [vmem],
        scratch_shapes=scratch,
        compiler_params=pltpu.CompilerParams(
            collective_id=1, has_side_effects=True, vmem_limit_bytes=63 * MIB
        ),
        name="back_and_reduce",
    )(*[given[name] for name in HBM_INPUTS + VMEM_INPUTS])
    return dict(zip(outs, result))


def shards(
    latents,
    pixels,
    crop_bounds,
    key_mask,
    query_gain,
    pixel_gain,
    cross_gain,
    attend_gain,
    feed_gain,
    query_weight,
    key_weight,
    value_weight,
    cross_out,
    cross_up,
    cross_down,
    self_attend,
    self_out,
    self_up,
    self_down,
    cotangent,
):
    channels = pixels.shape[2]
    rows = pixels.shape[1]
    pixel_total = key_mask.shape[1]
    l, c, s, t = place()

    def cut(v, k, n, axis):
        return lax.dynamic_slice_in_dim(v, k * n, n, axis)

    pixel_high, pixel_inverse = norm_parts(pixels.astype(F32))
    pixel_low = (pixel_high * pixel_gain.astype(F32)).astype(B16)
    home = jnp.pad(jnp.swapaxes(pixel_low, 1, 2), ((0, 0), (0, PAD - channels), (0, 0)))
    positions = jnp.arange(pixel_total, dtype=jnp.int32)
    start, count = crop_bounds[0, 0], crop_bounds[0, 1]
    kept = (positions >= start) & (positions < start + count) & (key_mask[0] == 1)
    kept = jnp.swapaxes(kept.reshape(16, 2, rows), 0, 1).reshape(1, pixel_total).astype(F32)
    kept = jnp.broadcast_to(kept, (8, pixel_total))
    key_wide = jnp.pad(key_weight, ((0, PAD - channels), (0, 0)))
    value_wide = jnp.pad(value_weight, ((0, PAD - channels), (0, 0)))
    shared = {
        "query_weight": query_weight,
        "key_wide": key_wide,
        "value_wide": value_wide,
        "cross_out": cross_out,
        "cross_up": cross_up,
        "cross_down": cross_down,
        "query_gain": query_gain.astype(F32)[None],
        "cross_gain": cross_gain.astype(F32)[None],
        "attend_gain": attend_gain.astype(F32)[None],
    }
    given = front(
        shared
        | {
            "home": home,
            "kept": kept,
            "latents": latents[0],
            "cotangent": cotangent[0],
            "self_attend": self_attend,
            "self_out": self_out,
            "self_up": self_up,
            "self_down": self_down,
            "feed_gain": feed_gain.astype(F32)[None],
        }
    )
    given = shared | given
    given["latents"] = given.pop("latents_turned")
    given["pixel_gain"] = jnp.pad(pixel_gain.astype(F32), (0, PAD - channels), constant_values=1.0)[None]
    done = back_and_reduce(given)
    picture_home, gains = done["home"], done["out_gains"]
    latents_out, latents_grad = done["latents_home"], done["latgrad_home"]
    out_s = done["out_S"].reshape(64, 2, 6, 256)
    heads_sums = [out_s[:, :, k].reshape(64, 512).astype(F32) for k in range(6)]
    out_p = done["out_P"].reshape(32, 2, 2, 512)
    out_q = done["out_Q"].reshape(32, 2, 2, 512)
    late_sum = out_q[:, :, 1].reshape(32, 1024)

    pixel_grad = jnp.swapaxes(picture_home[:, :channels], 1, 2).astype(F32)
    a = pixel_grad * pixel_gain.astype(F32)
    pixels_grad = (
        a
        - jnp.mean(a, axis=-1, keepdims=True)
        - pixel_high * jnp.mean(a * pixel_high, axis=-1, keepdims=True)
    ) * pixel_inverse

    queryweight_grad = dot(late_sum[:, :PAD], key_wide)
    keyweight_grad = late_sum[:, 512 : 512 + channels].astype(F32).T
    valueweight_grad = jnp.concatenate(
        [late_sum[:, 384:512], late_sum[:, 896:], late_sum[:, PAD : PAD + channels - 256]], axis=1
    ).astype(F32).T
    gain_sums = cut(gains[:4], 2 * s + t, 32, 1)
    return (
        latents_out[None],
        latents_grad.astype(F32)[None],
        pixels_grad,
        gain_sums[0],
        gains[4, :channels],
        gain_sums[1],
        gain_sums[2],
        gain_sums[3],
        queryweight_grad,
        keyweight_grad,
        valueweight_grad,
        out_q[:, :, 0].reshape(32, 1024).astype(F32),
        out_p[:, :, 1].reshape(32, 1024).astype(F32),
        out_p[:, :, 0].reshape(32, 1024).astype(F32),
        jnp.stack(heads_sums[3:]),
        heads_sums[2].T,
        heads_sums[1],
        heads_sums[0].T,
    )


def solution(mesh):
    in_specs = (
        P(("batch", "seq"), "tensor", None),
        P("batch", ("seq", "tensor"), None),
        P(("batch", "seq"), None),
        P(("batch", "seq"), None),
        P(),
        P(),
        P(),
        P(),
        P(),
        P(),
        P(),
        P(),
        P(),
        P(),
        P(),
        P(None, None, "tensor"),
        P("tensor", None),
        P(None, "tensor"),
        P("tensor", None),
        P(("batch", "seq"), "tensor", None),
    )
    out_specs = (
        P(("batch", "seq"), "tensor", None),
        P(("batch", "seq"), "tensor", None),
        P("batch", ("seq", "tensor"), None),
        P(("seq", "tensor")),
        P(),
        P(("seq", "tensor")),
        P(("seq", "tensor")),
        P(("seq", "tensor")),
        P(("seq", "tensor"), None),
        P(None, ("seq", "tensor")),
        P(None, ("seq", "tensor")),
        P(("seq", "tensor"), None),
        P(("seq", "tensor"), None),
        P(("seq", "tensor"), None),
        P(None, "seq", "tensor"),
        P("tensor", "seq"),
        P("seq", "tensor"),
        P("tensor", "seq"),
    )
    return jax.shard_map(shards, mesh=mesh, in_specs=in_specs, out_specs=out_specs, check_vma=False)
```

profile of v0, /device:TPU:1, one launch (start us, length us, event | category | flops | bytes accessed | tf_op | source)
XLA Modules:
  0.0 247.0 jit_solution(5977322403774218275)
XLA Ops:
  0.7 0.0 copy-start
  0.7 1.5 convert_reduce_fusion
  2.2 1.6 fusion.9
  3.8 0.0 copy-start.15
  3.8 0.0 copy-start.8
  3.8 0.4 fusion.10
  4.3 0.0 copy-start.4
  4.3 0.0 copy-start.13
  4.3 1.1 pad.15.refs_0_
  5.4 0.6 fusion.22
  7.3 0.1 compare_reduce_fusion
  7.4 0.7 fusion.19
  8.1 0.7 broadcast_in_dim.43.refs_1_
  8.7 0.8 pad.16.refs_9_.refs_26_
  9.6 0.8 pad.17.refs_10_.refs_27_
  10.4 0.6 broadcast_in_dim.56
  11.0 0.6 broadcast_in_dim.57
  11.6 0.6 broadcast_in_dim.58
  12.2 0.6 broadcast_in_dim.59
  12.8 98.8 %front.1 = (bf16[256,1024]{1,0:T(8,128)(2,1)}, bf16[256,1024]{1,0:T(8,128)(2,1)}, bf16[256,1024]{1,0:T(8,128)(2,1)}, bf16[256,1024]{1,0:T(8,128)(2,1)}, bf16[512...) custom-call(bf16[16,272,128]{2,1,0:T(8,128)(2,1)} %pad.15.refs_0_, ...), custom_call_target="tpu_custom_call" | custom-call | tf_op jit(solution)/shard_map/front/pallas_call | solution.py:648
  111.6 0.6 broadcast_in_dim.52.refs_38_
  112.2 115.1 %back_and_reduce.1 = (bf16[64,3072]{1,0:T(8,128)(2,1)}, bf16[32,2048]{1,0:T(8,128)(2,1)}, bf16[32,2048]{1,0:T(8,128)(2,1)}, bf16[16,272,128]{2,1,0:T(8,128)(2,1)...) custom-call(bf16[256,1024]{1,0:T(8,128)(2,1)} %get-tuple-element.55.refs_0_, ...), custom_call_target="tpu_custom_call" | custom-call | tf_op jit(solution)/shard_map/back_and_reduce/pallas_call | solution.py:1249
  227.4 1.6 reshape.132
  229.0 1.1 slice_reduce_fusion.2
  230.2 0.8 maximum_convert_fusion
  231.0 1.0 reshape.130
  232.0 0.4 slice_reduce_fusion.3
  232.5 0.1 slice.101
  232.5 0.6 convert_bitcast_fusion
  233.2 0.8 bitcast_reduce_fusion
  234.0 0.8 fusion.8
  234.7 1.7 copy.43
  236.5 1.2 fusion.11
  237.7 0.7 copy.49
  238.4 0.7 copy.51
  239.0 0.7 copy.50
  239.7 1.1 bitcast_convert_fusion
  240.8 0.1 reshape.131
  240.9 0.8 fusion.14
  241.7 0.7 copy.47
  242.3 0.7 copy.48
  243.0 0.4 fusion.16
  243.4 0.7 copy.46
  244.1 0.9 fusion.17
  245.0 0.1 constant_dynamic-slice_fusion
  245.1 0.5 slice_bitcast_fusion
  245.6 0.6 slice_reduce_fusion.4
  246.2 0.8 copy.58
  (40 shorter events, 0.3 us)
Async XLA Ops:
  0.7 3.1 %copy-start = (bf16[16,128,261]{1,0,2:T(8,128)(2,1)S(1)}, bf16[16,128,261]{1,0,2:T(8,128)(2,1)}, u32[]{:S(2)}) copy-start(bf16[16,128,261]{1,0,2:T(8,128)(2,1)} %param.21) | copy-start | bytes 3207172
  0.7 3.1 %copy-start.10 = (bf16[261]{0:T(512)(128)(2,1)S(1)}, bf16[261]{0:T(512)(128)(2,1)}, u32[]{:S(2)}) copy-start(bf16[261]{0:T(512)(128)(2,1)} %param.25) | copy-start | bytes 1570
  3.8 1.6 copy-start.15
  3.8 3.5 %copy-start.8 = (s32[1,4096]{1,0:T(1,128)S(1)}, s32[1,4096]{1,0:T(1,128)}, u32[]{:S(2)}) copy-start(s32[1,4096]{1,0:T(1,128)} %param.23) | copy-start | bytes 49156
  3.8 4.9 %copy-start.3 = (bf16[261,1024]{1,0:T(8,128)(2,1)S(1)}, bf16[261,1024]{1,0:T(8,128)(2,1)}, u32[]{:S(2)}) copy-start(bf16[261,1024]{1,0:T(8,128)(2,1)} %param.30) | copy-start | bytes 1603588
  4.3 5.3 %copy-start.4 = (bf16[261,1024]{1,0:T(8,128)(2,1)S(1)}, bf16[261,1024]{1,0:T(8,128)(2,1)}, u32[]{:S(2)}) copy-start(bf16[261,1024]{1,0:T(8,128)(2,1)} %param.31) | copy-start | bytes 1603588
  4.3 6.1 %copy-start.11 = (bf16[1024]{0:T(1024)(128)(2,1)S(1)}, bf16[1024]{0:T(1024)(128)(2,1)}, u32[]{:S(2)}) copy-start(bf16[1024]{0:T(1024)(128)(2,1)} %param.24) | copy-start | bytes 6148
  4.3 6.7 %copy-start.12 = (bf16[1024]{0:T(1024)(128)(2,1)S(1)}, bf16[1024]{0:T(1024)(128)(2,1)}, u32[]{:S(2)}) copy-start(bf16[1024]{0:T(1024)(128)(2,1)} %param.26) | copy-start | bytes 6148
  4.3 7.3 %copy-start.13 = (bf16[1024]{0:T(1024)(128)(2,1)S(1)}, bf16[1024]{0:T(1024)(128)(2,1)}, u32[]{:S(2)}) copy-start(bf16[1024]{0:T(1024)(128)(2,1)} %param.27) | copy-start | bytes 6148
  4.3 7.9 %copy-start.14 = (bf16[1024]{0:T(1024)(128)(2,1)S(1)}, bf16[1024]{0:T(1024)(128)(2,1)}, u32[]{:S(2)}) copy-start(bf16[1024]{0:T(1024)(128)(2,1)} %param.28) | copy-start | bytes 6148
  227.3 5.8 %copy-start.1 = (bf16[16,128,261]{1,0,2:T(8,128)(2,1)S(1)}, bf16[16,128,261]{1,0,2:T(8,128)(2,1)}, u32[]{:S(2)}) copy-start(bf16[16,128,261]{1,0,2:T(8,128)(2,1)} %param.21) | copy-start | bytes 3207172
  227.4 5.8 %copy-start.2 = (bf16[16,272,128]{2,1,0:T(8,128)(2,1)S(1)}, bf16[16,272,128]{2,1,0:T(8,128)(2,1)}, u32[]{:S(2)}) copy-start(bf16[16,272,128]{2,1,0:T(8,128)(2,1)} %get-tuple-element.87) | copy-start | bytes 3342340
  234.7 5.0 %copy-start.5 = (bf16[256,1024]{1,0:T(8,128)(2,1)S(1)}, bf16[256,1024]{1,0:T(8,128)(2,1)}, u32[]{:S(2)}) copy-start(bf16[256,1024]{1,0:T(8,128)(2,1)} %get-tuple-element.86) | copy-start | bytes 1572868
  236.5 4.3 %copy-start.7 = (bf16[32,2048]{1,0:T(8,128)(2,1)S(1)}, bf16[32,2048]{1,0:T(8,128)(2,1)}, u32[]{:S(2)}) copy-start(bf16[32,2048]{1,0:T(8,128)(2,1)} %get-tuple-element.90) | copy-start | bytes 393220
  239.0 6.0 %copy-start.9 = (f32[8,1024]{1,0:T(8,128)S(1)}, f32[8,1024]{1,0:T(8,128)}, u32[]{:S(2)}) copy-start(f32[8,1024]{1,0:T(8,128)} %get-tuple-element.88) | copy-start | bytes 98308
  239.7 6.5 %copy-start.6 = (bf16[256,1024]{1,0:T(8,128)(2,1)S(1)}, bf16[256,1024]{1,0:T(8,128)(2,1)}, u32[]{:S(2)}) copy-start(bf16[256,1024]{1,0:T(8,128)(2,1)} %get-tuple-element.85) | copy-start | bytes 1572868
where the time goes:
time: 248 us; the launch traced here: 247 us
  Pallas kernels  214 us (86%)
  local copies, waits for them, and re-layouts  16.8 us (7%)
  other arithmetic  13.1 us (5%)
    pallas_call x1, Pallas kernels, back_and_reduce(): pl.pallas_call(functools.partial(back_kernel, tuple(names), sems), out_sh...  115 us
    pallas_call x1, Pallas kernels, front(): pl.pallas_call(functools.partial(front_kernel, tuple(names), sems), out_s...  98.8 us
    unnamed x41, local copies, waits for them, and re-layouts  6.64 us

commit v1 on v0

v1 whole, which is shorter than its diff:
```python
import functools
import math

import jax
import jax.numpy as jnp
from jax import lax
from jax.experimental import pallas as pl
from jax.experimental.pallas import tpu as pltpu
from jax.sharding import PartitionSpec as P

HEAD_WIDTH = 128
EPS = 1e-05
MASKED = -1000000000.0
MESH = pl.DeviceIdType.MESH
F32 = jnp.float32
B16 = jnp.bfloat16
LANES = 128
PAD = 272
WIDE = 1024
CYCLE = ("XA", "XB", "ZA", "ZB", "T")

def norm_parts(values):
    average = jnp.mean(values, axis=-1, keepdims=True)
    centered = values - average
    spread = jnp.mean(centered * centered, axis=-1, keepdims=True)
    inverse = lax.rsqrt(spread + EPS)
    return centered * inverse, inverse


def dot(a, b):
    return jnp.dot(a, b, preferred_element_type=F32)


def dot_t(a, b):
    return lax.dot_general(a, b, (((1,), (1,)), ((), ())), preferred_element_type=F32)


def tdot(a, b):
    return lax.dot_general(a, b, (((0,), (0,)), ((), ())), preferred_element_type=F32)


def flip(p):
    return p + 1 - 2 * lax.rem(p, 2)


def place():
    b, s, t = lax.axis_index("batch"), lax.axis_index("seq"), lax.axis_index("tensor")
    return lax.div(b, 2), lax.rem(b, 2), s, t


MIB = 1024 * 1024
ROWS = 256
GELU_K = math.sqrt(2.0 / math.pi)


def gelu(u):
    return 0.5 * u * (1.0 + jnp.tanh(GELU_K * (u + 0.044715 * u * u * u)))


def gelu_slope(u):
    th = jnp.tanh(GELU_K * (u + 0.044715 * u * u * u))
    return 0.5 * (1.0 + th) + 0.5 * u * (1.0 - th * th) * GELU_K * (1.0 + 3.0 * 0.044715 * u * u)


def loop(n, step):
    lax.fori_loop(0, n, lambda i, carry: (step(i), carry)[1], 0)


def block(i, n):
    return pl.ds(pl.multiple_of(i * n, n), n)


FRONT_HBM = (
    ("pixels", "latents", "cotangent", "self_attend", "self_out", "self_up", "self_down")
    + ("query_weight", "cross_out", "cross_up", "cross_down")
)
FRONT_VMEM = ("norm_gains", "pixel_gain", "key_weight", "value_weight", "key_mask", "crop_bounds")
FRONT_OUT = {
    "cot": ((512, WIDE), B16),
    "cross_act": ((512, WIDE), B16),
    "cross_in": ((512, WIDE), B16),
    "attended": ((512, WIDE), B16),
    "late_x": ((512, WIDE), B16),
    "mixed_pixels": ((512, 512), B16),
    "mixed": ((512, 512), B16),
    "attend_in": ((512, WIDE), B16),
    "projected": ((3, 512, 512), B16),
    "probs": ((8, ROWS, 512), B16),
    "out_mine": ((512, WIDE), B16),
    "attend_far": ((3, WIDE, 256), B16),
    "up_far": ((WIDE, 512), B16),
    "down_far": ((512, WIDE), B16),
    "after_mlp": ((ROWS, WIDE), F32),
    "after_attend": ((ROWS, WIDE), F32),
    "cross_hidden": ((ROWS, WIDE), F32),
    "after_cross": ((ROWS, WIDE), F32),
    "latents_turned": ((ROWS, WIDE), B16),
    "picture": ((PAD, 4096), B16),
    "raised": ((8, ROWS, 512), B16),
    "mixed_f32": ((ROWS, PAD), F32),
    "asked": ((ROWS, PAD), B16),
    "key_wide": ((PAD, WIDE), B16),
    "value_wide": ((PAD, WIDE), B16),
    "inverse_total": ((ROWS, 1), F32),
    "any_kept": ((1, 1), F32),
}
FRONT_OUT_VMEM = ("inverse_total", "any_kept")


def front_kernel(names, sems, *refs):
    l, c, s, t = place()
    seq = 16
    r = dict(zip(names, refs))
    send, recv, local = r["send"], r["recv"], r["local"]
    cross_scale = 1.0 / math.sqrt(WIDE)
    self_scale = 1.0 / math.sqrt(HEAD_WIDTH)
    sib = (2 * l + 1 - c, s, t)
    over = (2 * (1 - l) + c, s, 1 - t)
    beside = (2 * (1 - l) + c, s, t)

    def peer(k):
        return (2 * l + t, lax.rem(s + k, seq), c)

    barrier = pltpu.get_barrier_semaphore()
    for device in (sib, over, beside):
        pl.semaphore_signal(barrier, inc=1, device_id=device, device_id_type=MESH)
    def plane(k):
        return (2 * l + c, lax.rem(s + k, seq), t)

    for k in range(1, seq):
        pl.semaphore_signal(barrier, inc=1, device_id=peer(k), device_id_type=MESH)
        pl.semaphore_signal(barrier, inc=1, device_id=plane(k), device_id_type=MESH)

    @pl.when(c != t)
    def _():
        pl.semaphore_signal(barrier, inc=1, device_id=peer(0), device_id_type=MESH)
        pl.semaphore_wait(barrier, 2 + 2 * seq)

    @pl.when(c == t)
    def _():
        pl.semaphore_wait(barrier, 1 + 2 * seq)

    used = [0, 0]
    waits, stores = [], []

    def remote_of(src, dst, device):
        i = used[0]
        used[0] += 1
        return pltpu.make_async_remote_copy(
            src_ref=src, dst_ref=dst, send_sem=send.at[i], recv_sem=recv.at[i], device_id=device, device_id_type=MESH
        )

    def remote(src, dst, device):
        copy = remote_of(src, dst, device)
        copy.start()
        waits.append(copy)
        return copy

    def here_of(src, dst):
        i = used[1]
        used[1] += 1
        return pltpu.make_async_copy(src, dst, local.at[i])

    def here(src, dst):
        copy = here_of(src, dst)
        copy.start()
        return copy

    def store(name, src):
        stores.append(here(src, r[name]))

    top, low = pl.ds(0, ROWS), pl.ds(ROWS, ROWS)
    shared = []

    def share(name, src, give=None):
        stores.append(here(src, r[name].at[top]))
        shared.append(remote(src if give is None else give, r[name].at[low], sib))

    ready = {}

    def await_all(*wanted):
        for name in wanted:
            for wait in ready.pop(name, ()):
                wait()

    base = pl.multiple_of(c * (seq * LANES), LANES)
    far = pl.multiple_of(t * (seq * LANES), LANES)
    picture = r["v_picture"]

    def away_of(k):
        return remote_of(
            r["v_home"].at[lax.rem(s + k, seq)],
            picture.at[:, pl.ds(pl.multiple_of(far + s * LANES, LANES), LANES)],
            peer(k),
        )

    away = [away_of(k) for k in range(seq)]
    lat_move, cot_move = remote_of(r["latents"], r["v_lat"], peer(0)), remote_of(r["cotangent"], r["v_cot"], peer(0))
    kept_move = remote_of(r["v_kept_own"], r["v_kept"], sib)
    lat_stay, cot_stay = here_of(r["latents"], r["v_lat"]), here_of(r["cotangent"], r["v_cot"])
    kept_stay = here_of(r["v_kept_own"], r["v_kept"])
    picture_stay = here_of(r["v_home"].at[s], picture.at[:, pl.ds(pl.multiple_of(base + s * LANES, LANES), LANES)])

    @pl.when(c != t)
    def _():
        lat_move.start()

    @pl.when(c == t)
    def _():
        lat_stay.start()
        cot_stay.start()

    pixels_copy = here(r["pixels"], r["v_pixels"])

    mine, theirs = l, 1 - l
    own256 = 256 * c
    own_columns = pl.ds(pl.multiple_of(own256, LANES), 256)
    attend_far, out_w, up_far, down_far = r["w_attend_far"], r["w_out"], r["w_up_far"], r["w_down_far"]
    left = pl.ds(0, 256)

    def rows16(base_row, piece):
        return pl.ds(pl.multiple_of(base_row + 16 * piece, 16), 16)

    shares = {
        "out": (lambda p: r["self_out"].at[rows16(own256, p)], lambda p: out_w.at[rows16(256, p)]),
        "up": (lambda p: r["self_up"].at[block(p, 64), own_columns], lambda p: up_far.at[block(p, 64), left]),
        "down": (lambda p: r["self_down"].at[rows16(own256, p)], lambda p: down_far.at[rows16(0, p)]),
    }
    first_piece = {name: remote(src(s), dst(s), over) for name, (src, dst) in shares.items()}

    def attend_piece(k, p):
        return attend_far.at[k, block(p, 512)]

    across = {}
    for k in range(3):
        across["attend%d" % k] = remote(
            r["self_attend"].at[k, block(theirs, 512), own_columns], attend_piece(k, theirs), over
        )
    onward = {}

    def pass_on(*wanted):
        for name in wanted:
            across[name].wait_recv()
            k = int(name[-1])
            onward[name] = remote(attend_piece(k, mine), attend_piece(k, mine), beside)

    def pass_rest(*wanted):
        for name in wanted:
            onward[name].wait_recv()

    pieces = {}

    def spread_pieces(*wanted):
        for name in wanted:
            first_piece[name].wait_recv()
            dst = shares[name][1]
            pieces[name] = [remote(dst(s), dst(s), plane(k)) for k in range(1, seq)]

    whole = {
        "out": (out_w.at[pl.ds(256, 256)], out_w.at[pl.ds(768, 256)]),
        "up": (up_far.at[:, left], up_far.at[:, pl.ds(256, 256)]),
        "down": (down_far.at[left], down_far.at[pl.ds(256, 256)]),
    }
    sib_quarter = {}

    def gather_pieces(*wanted):
        for name in wanted:
            for copy in pieces[name]:
                copy.wait_recv()
            sib_quarter[name] = remote(*whole[name], sib)

    def arrived(*wanted):
        for name in wanted:
            sib_quarter[name].wait_recv()

    @pl.when(c != t)
    def _():
        cot_move.start()

    pixels_copy.wait()
    pixels, normed = r["v_pixels"], r["v_normed"]
    channels = pixels.shape[0]
    some = 9

    def features(i):
        return pl.ds(i * some, some)

    def sum_step(i, total):
        return total + jnp.sum(pixels[features(i)].astype(F32), axis=0)

    zeros = jnp.zeros(pixels.shape[1:], F32)
    average = lax.fori_loop(0, channels // some, sum_step, zeros) * (1.0 / channels)

    def square_step(i, total):
        centered = pixels[features(i)].astype(F32) - average
        return total + jnp.sum(centered * centered, axis=0)

    spread = lax.fori_loop(0, channels // some, square_step, zeros) * (1.0 / channels)
    inverse = lax.rsqrt(spread + EPS)

    def norm_step(i):
        value = (pixels[features(i)].astype(F32) - average) * inverse * r["pixel_gain"][features(i)]
        normed[pl.ds(pl.multiple_of(i * (some * 16), 16), some * 16), :] = value.reshape(some * 16, LANES)

    loop(channels // some, norm_step)
    normed[channels * 16 :, :] = jnp.zeros(((PAD - channels) * 16, LANES), F32)

    def turn_image(k):
        image = lax.rem(s + k, seq)
        r["v_home"][image] = normed[pl.ds(image, PAD, stride=16), :].astype(B16)

    turn_image(0)

    @pl.when(c != t)
    def _():
        away[0].start()

    @pl.when(c == t)
    def _():
        picture_stay.start()

    for k in range(1, seq):
        turn_image(k)
        away[k].start()

    start, count = r["crop_bounds"][:, 0:1], r["crop_bounds"][:, 1:2]
    lanes = lax.broadcasted_iota(jnp.int32, (1, LANES), 1)
    for k in range(2 * seq):
        row = lanes + k * LANES
        keep = (row >= start) & (row < start + count) & (r["key_mask"][:, pl.ds(k * LANES, LANES)] == 1)
        to = pl.ds(((k % 2) * seq + k // 2) * LANES, LANES)
        r["v_kept_own"][:, to] = jnp.broadcast_to(jnp.where(keep, 1.0, 0.0), (8, LANES))

    @pl.when(c == t)
    def _():
        kept_stay.start()
        kept_move.start()

    for name in ("key", "value"):
        ref, to = r[name + "_weight"], r["w_" + name]
        to[:256, :] = ref[:256, :]
        to[256:, :] = jnp.concatenate(
            [ref[256:channels, :].astype(F32), jnp.zeros((PAD - channels, WIDE), F32)], axis=0
        ).astype(B16)
        store(name + "_wide", to)
    for name, to in (
        ("query_weight", "w_query"),
        ("cross_out", "w_cross_out"),
        ("cross_up", "w_cross_up"),
        ("cross_down", "w_cross_down"),
    ):
        ready[to] = [here(r[name], r[to]).wait]
    ready["attend_own"] = [here(r["self_attend"].at[:, :, own_columns], r["w_attend_own"]).wait]
    ready["out_own"] = [
        here(r["self_out"].at[pl.ds(pl.multiple_of(own256, LANES), 256)], out_w.at[pl.ds(0, 256)]).wait,
        here(r["self_out"].at[pl.ds(pl.multiple_of(256 - own256, LANES), 256)], out_w.at[pl.ds(512, 256)]).wait,
    ]

    spread_pieces("out", "up", "down")

    def norm_rows(value_ref, gain, out_ref, also=None):
        def step(i):
            rows = block(i, 64)
            v = value_ref[rows, :].astype(F32)
            high, _ = norm_parts(v)
            out_ref[rows, :] = (high * gain).astype(B16)

        loop(ROWS // 64, step)

    def each256(n, step):
        loop(n // 256, lambda i: step(block(i, 256)))

    @pl.when(c != t)
    def _():
        lat_move.wait_recv()

    @pl.when(c == t)
    def _():
        lat_stay.wait()

    store("latents_turned", r["v_lat"])
    query_low, queries = r["v_query_low"], r["v_queries"]
    norm_rows(r["v_lat"], r["norm_gains"][0:1, :], query_low)
    await_all("w_query")

    def query_step(columns):
        queries[:, columns] = dot(query_low[...], r["w_query"][:, columns]).astype(B16)

    each256(WIDE, query_step)
    r["v_asked"][...] = (dot_t(queries[...], r["w_key"][...]) * cross_scale).astype(B16)
    store("asked", r["v_asked"])
    late = r["late_x"]
    late_keep = [here_of(src, late.at[top]) for src in (query_low, queries)]
    late_give = [remote_of(src, late.at[low], sib) for src in (queries, query_low)]

    @pl.when(c == 0)
    def _():
        late_keep[0].start()
        late_give[0].start()

    @pl.when(c == 1)
    def _():
        late_keep[1].start()
        late_give[1].start()

    def chunk(k):
        return picture.at[:, pl.ds(pl.multiple_of(base + lax.rem(s - k + seq, seq) * LANES, LANES), LANES)]

    @pl.when(c != t)
    def _():
        away[0].wait_recv()
        kept_move.wait_recv()

    @pl.when(c == t)
    def _():
        picture_stay.wait()
        kept_stay.wait()

    passed = [remote(chunk(0), chunk(0), sib)]
    for k in range(1, seq):
        away[k].wait_recv()
        passed.append(remote(chunk(k), chunk(k), sib))
    for copy in passed:
        copy.wait_recv()
    store("picture", picture)

    scores, raised = r["v_scores"], r["v_raised"]
    r["v_top"][...] = jnp.full((ROWS, 1), -3.0e38, F32)
    r["v_total"][...] = jnp.zeros((ROWS, 1), F32)
    r["v_mixed"][...] = jnp.zeros_like(r["v_mixed"])
    r["any_kept"][...] = jnp.max(r["v_kept"][0:1, :], axis=-1, keepdims=True)

    def score_step(i):
        columns = block(i, 512)
        value = dot(r["v_asked"][...], picture[:, columns])
        value = jnp.where(r["v_kept"][0:1, columns] > 0.5, value, MASKED)
        scores[:, columns] = value
        r["v_top"][...] = jnp.maximum(r["v_top"][...], jnp.max(value, axis=-1, keepdims=True))

    loop(8, score_step)

    def raise_step(i):
        columns = block(i, 512)
        value = jnp.exp(scores[:, columns] - r["v_top"][...])
        r["v_total"][...] += jnp.sum(value, axis=-1, keepdims=True)
        value = value.astype(B16)
        raised[i] = value
        r["v_mixed"][...] += dot_t(value, picture[:, columns])

    loop(8, raise_step)
    store("raised", raised)
    inverse_total = 1.0 / r["v_total"][...]
    r["inverse_total"][...] = inverse_total
    mixed = r["v_mixed"][...] * inverse_total
    r["v_mixed"][...] = mixed
    store("mixed_f32", r["v_mixed"])
    r["v_mixed_wide"][...] = jnp.zeros_like(r["v_mixed_wide"])
    r["v_mixed_wide"][:, :PAD] = mixed
    tail = pltpu.roll(r["v_mixed_wide"][:, 256:384], 16, 1).astype(B16)
    for name, core in (("mixed_pixels", c), ("mixed_pixels_give", 1 - c)):
        ref = r["v_" + name]
        ref[:, :256] = jnp.zeros((ROWS, 256), B16)
        ref[:, 256:384] = tail
        ref[:, 384:] = r["v_mixed_wide"][:, pl.ds(pl.multiple_of(LANES * core, LANES), LANES)].astype(B16)
    share("mixed_pixels", r["v_mixed_pixels"], r["v_mixed_pixels_give"])
    await_all("w_cross_out")
    r["v_attended"][...] = dot(mixed.astype(B16), r["w_value"][...]).astype(B16)
    share("attended", r["v_attended"])

    def out_step(columns):
        r["v_after_cross"][:, columns] = r["v_lat"][:, columns].astype(F32) + dot(
            r["v_attended"][...], r["w_cross_out"][:, columns]
        )

    each256(WIDE, out_step)
    store("after_cross", r["v_after_cross"])
    pass_on("attend0")
    norm_rows(r["v_after_cross"], r["norm_gains"][1:2, :], r["v_cross_in"])
    share("cross_in", r["v_cross_in"])
    await_all("w_cross_up", "w_cross_down")

    def up_step(columns):
        hidden = dot(r["v_cross_in"][...], r["w_cross_up"][:, columns])
        r["v_hidden"][:, columns] = hidden
        r["v_cross_act"][:, columns] = gelu(hidden).astype(B16)

    each256(WIDE, up_step)
    store("cross_hidden", r["v_hidden"])
    share("cross_act", r["v_cross_act"])
    pass_on("attend1")

    def down_step(columns):
        r["v_after_mlp"][:, columns] = r["v_after_cross"][:, columns] + dot(
            r["v_cross_act"][...], r["w_cross_down"][:, columns]
        )

    each256(WIDE, down_step)
    store("after_mlp", r["v_after_mlp"])

    attend_in = r["v_attend_in"]
    norm_rows(r["v_after_mlp"], r["norm_gains"][2:3, :], attend_in)
    attend_copy = remote(attend_in.at[top], attend_in.at[low], sib)
    await_all("attend_own")
    pass_on("attend2")
    attend_copy.wait_recv()
    store("attend_in", attend_in)
    projected, probs = r["v_projected"], r["v_probs"]

    def project(weights, at):
        for k in range(3):
            projected[k, :, pl.ds(at, 256)] = dot(attend_in[...], weights[k]).astype(B16)

    def attend(h):
        columns = block(h, HEAD_WIDTH)
        dotted = dot_t(projected[0, :, columns], projected[1, :, columns]) * self_scale
        value = jnp.exp(dotted - jnp.max(dotted, axis=-1, keepdims=True))
        value = (value * (1.0 / jnp.sum(value, axis=-1, keepdims=True))).astype(B16)
        probs[2 * h] = value[:ROWS]
        probs[2 * h + 1] = value[ROWS:]
        r["v_self"][:, columns] = dot(value, projected[2, :, columns]).astype(B16)

    project(r["w_attend_own"], 0)
    loop(2, attend)
    pass_rest("attend0", "attend1", "attend2")
    project(attend_far, 256)
    loop(2, lambda i: attend(i + 2))
    store("mixed", r["v_self"])
    self_copy = remote(r["v_self"].at[low], r["v_self_in"], sib)
    store("projected", projected)
    store("probs", probs)
    store("attend_far", attend_far)

    @pl.when(c != t)
    def _():
        cot_move.wait_recv()

    @pl.when(c == t)
    def _():
        cot_stay.wait()

    share("cot", r["v_cot"])
    gather_pieces("out")
    await_all("out_own")
    arrived("out")
    store("out_mine", out_w.at[pl.ds(0, 512)])
    self_copy.wait_recv()

    def attended_step(columns):
        r["v_after_attend"][:, columns] = (
            r["v_after_mlp"][:, columns]
            + dot(r["v_self"][top, :], out_w[pl.ds(0, 512), columns])
            + dot(r["v_self_in"][...], out_w[pl.ds(512, 512), columns])
        )

    each256(WIDE, attended_step)
    store("after_attend", r["v_after_attend"])
    gather_pieces("up", "down")
    arrived("up", "down")
    store("up_far", up_far)
    store("down_far", down_far)

    @pl.when(c != t)
    def _():
        lat_move.wait_send()
        cot_move.wait_send()
        away[0].wait_send()

    @pl.when(c == t)
    def _():
        kept_move.wait_send()

    @pl.when(c == 0)
    def _():
        late_keep[0].wait()
        late_give[0].wait_send()
        late_give[1].wait_recv()

    @pl.when(c == 1)
    def _():
        late_keep[1].wait()
        late_give[1].wait_send()
        late_give[0].wait_recv()

    for k in range(1, seq):
        away[k].wait_send()
    for copy in shared:
        copy.wait_recv()
    for copy in waits:
        copy.wait_send()
    for copy in stores:
        copy.wait()
    assert not ready, tuple(ready)
    assert used[0] <= sems[0] and used[1] <= sems[1], used


def front(given):
    names, scratch = [], []

    def room(name, shape, dtype=B16):
        names.append(name)
        scratch.append(pltpu.VMEM(shape, dtype))

    sems = (101, 38)
    names += list(FRONT_HBM) + list(FRONT_VMEM) + list(FRONT_OUT)
    for name in ("send", "recv", "local"):
        names.append(name)
        scratch.append(pltpu.SemaphoreType.DMA((sems[1 if name == "local" else 0],)))
    for name in ("query", "cross_out", "cross_up", "cross_down", "out"):
        room("w_" + name, (WIDE, WIDE))
    for name in ("key", "value"):
        room("w_" + name, (PAD, WIDE))
    for name in ("attend_own", "attend_far"):
        room("w_" + name, (3, WIDE, 256))
    room("w_up_far", (WIDE, 512))
    room("w_down_far", (512, WIDE))
    room("v_picture", (PAD, 4096))
    room("v_pixels", (261, 16, LANES))
    room("v_normed", (PAD * 16, LANES), F32)
    room("v_home", (16, PAD, LANES))
    room("v_kept", (8, 4096), F32)
    room("v_kept_own", (8, 4096), F32)
    room("v_scores", (ROWS, 4096), F32)
    room("v_raised", (8, ROWS, 512))
    for name in ("lat", "cot", "query_low", "queries", "attended", "cross_in", "cross_act"):
        room("v_" + name, (ROWS, WIDE))
    for name in ("after_cross", "hidden", "after_mlp", "after_attend"):
        room("v_" + name, (ROWS, WIDE), F32)
    room("v_attend_in", (512, WIDE))
    room("v_projected", (3, 512, 512))
    room("v_probs", (8, ROWS, 512))
    room("v_self", (512, 512))
    room("v_self_in", (ROWS, 512))
    room("v_asked", (ROWS, PAD))
    room("v_top", (ROWS, 1), F32)
    room("v_total", (ROWS, 1), F32)
    room("v_mixed", (ROWS, PAD), F32)
    room("v_mixed_wide", (ROWS, 384), F32)
    room("v_mixed_pixels", (ROWS, 512))
    room("v_mixed_pixels_give", (ROWS, 512))
    anywhere = pl.BlockSpec(memory_space=pl.ANY)
    vmem = pl.BlockSpec(memory_space=pltpu.VMEM)
    result = pl.pallas_call(
        functools.partial(front_kernel, tuple(names), sems),
        out_shape=[jax.ShapeDtypeStruct(*spec) for spec in FRONT_OUT.values()],
        in_specs=[anywhere] * len(FRONT_HBM) + [vmem] * len(FRONT_VMEM),
        out_specs=[vmem if name in FRONT_OUT_VMEM else anywhere for name in FRONT_OUT],
        scratch_shapes=scratch,
        compiler_params=pltpu.CompilerParams(collective_id=0, has_side_effects=True, vmem_limit_bytes=63 * MIB),
        name="front",
    )(*[given[name] for name in FRONT_HBM + FRONT_VMEM])
    return dict(zip(FRONT_OUT, result))


LINKS = ("XA", "ZA", "L", "XB", "ZB", "O")
SETS = {"S": ((0, 1, 2, 3, 4, 5), 32), "P": ((0, 3, 1, 4), 16), "Q": ((2, 5, 0, 3), 16)}
BACK_HBM = (
    ("cot", "cross_act", "cross_in", "attended", "late_x", "mixed_pixels", "mixed", "attend_in", "projected", "probs")
    + ("out_mine", "attend_far", "up_far", "down_far", "after_mlp", "after_attend", "cross_hidden", "after_cross")
    + ("latents_turned", "picture", "raised", "mixed_f32", "asked", "self_attend", "self_up", "self_down")
    + ("cross_down", "cross_up", "cross_out", "query_weight", "key_wide", "value_wide")
)
BACK_VMEM = ("inverse_total", "any_kept", "norm_gains")
BACK_OUT = {
    "out_S": ((64, 2 * 6 * 256), B16),
    "out_P": ((32, 2 * 4 * 256), B16),
    "out_Q": ((32, 2 * 4 * 256), B16),
    "home": ((16, PAD, LANES), B16),
    "latents_home": ((ROWS, WIDE), B16),
    "latgrad_home": ((ROWS, WIDE), B16),
    "out_gains": ((8, WIDE), F32),
}


def back_kernel(names, sems, *refs):
    l, c, s, t = place()
    z, x = lax.div(s, 4), lax.rem(s, 4)
    seq = 16
    r = dict(zip(names, refs))
    send, recv, local = r["send"], r["recv"], r["local"]
    cross_scale = 1.0 / math.sqrt(WIDE)
    self_scale = 1.0 / math.sqrt(HEAD_WIDTH)

    partner = {
        "XA": (2 * l + c, z * 4 + flip(x), t),
        "XB": (2 * l + c, z * 4 + 3 - x, t),
        "ZA": (2 * l + c, flip(z) * 4 + x, t),
        "ZB": (2 * l + c, (3 - z) * 4 + x, t),
        "L": (2 * (1 - l) + c, s, t),
        "O": (2 * (1 - l) + c, s, 1 - t),
        "C": (2 * l + 1 - c, s, t),
        "D": (2 * (1 - l) + 1 - c, s, t),
    }

    def peer(k):
        return (2 * l + t, lax.rem(s + k, seq), c)

    barrier = pltpu.get_barrier_semaphore()
    for device in partner.values():
        pl.semaphore_signal(barrier, inc=1, device_id=device, device_id_type=MESH)
    for k in range(1, seq):
        pl.semaphore_signal(barrier, inc=1, device_id=peer(k), device_id_type=MESH)

    @pl.when(c != t)
    def _():
        pl.semaphore_signal(barrier, inc=1, device_id=peer(0), device_id_type=MESH)
        pl.semaphore_wait(barrier, len(partner) + seq)

    @pl.when(c == t)
    def _():
        pl.semaphore_wait(barrier, len(partner) + seq - 1)

    used = [0, 0]
    waits = []

    def remote_of(src, dst, device):
        i = used[0]
        used[0] += 1
        return pltpu.make_async_remote_copy(
            src_ref=src, dst_ref=dst, send_sem=send.at[i], recv_sem=recv.at[i], device_id=device, device_id_type=MESH
        )

    def remote(src, dst, device):
        copy = remote_of(src, dst, device)
        copy.start()
        waits.append(copy)
        return copy

    def sent(*copies):
        for copy in copies:
            copy.wait_send()
            waits[:] = [other for other in waits if other is not copy]

    def here_of(src, dst):
        i = used[1]
        used[1] += 1
        return pltpu.make_async_copy(src, dst, local.at[i])

    def here(src, dst):
        copy = here_of(src, dst)
        copy.start()
        return copy

    ready = {}

    def await_all(*wanted):
        for name in wanted:
            for wait in ready.pop(name):
                wait()

    def load(name, to, key=None):
        ready[key or name] = [here(r[name], to).wait]

    sib = partner["C"]
    top, low = pl.ds(0, ROWS), pl.ds(ROWS, ROWS)
    keep512 = pl.ds(pl.multiple_of(512 * c, LANES), 512)
    give512 = pl.ds(pl.multiple_of(512 * (1 - c), LANES), 512)
    keep256 = pl.ds(pl.multiple_of(256 * c, LANES), 256)
    give256 = pl.ds(pl.multiple_of(256 * (1 - c), LANES), 256)
    left, right = pl.ds(0, 256), pl.ds(256, 256)
    x1, x2, x3, x4, x5 = (r["x%d" % k] for k in range(1, 6))
    up_w, down_w, probs = r["w_up"], r["w_down"], r["v_probs"]

    load("after_attend", r["v_norm"])
    ready["up"] = [
        here(r["self_up"], up_w.at[:, pl.ds(0, 512)]).wait,
        here(r["up_far"], up_w.at[:, pl.ds(512, 512)]).wait,
    ]
    load("cot", x1)
    ready["down"] = [
        here(r["self_down"], down_w.at[pl.ds(0, 512)]).wait,
        here(r["down_far"], down_w.at[pl.ds(512, 512)]).wait,
    ]
    load("out_mine", r["w_out_mine"])
    load("projected", r["v_projected"])
    load("probs", probs)
    load("mixed", r["y_mixed"])
    ready["attend_own"] = [
        here(r["self_attend"].at[:, :, keep256], r["w_attend_own"]).wait
    ]
    load("attend_far", r["w_attend_far"])
    load("attend_in", x4)
    load("cross_hidden", r["v_hidden"])
    load("value_wide", r["w_value"])
    load("key_wide", r["w_key"])
    load("picture", r["v_picture"])
    load("mixed_f32", r["v_mixed"])
    load("asked", r["v_asked"])
    load("mixed_pixels", r["y_mixed_pixels"])

    class Part:
        def __init__(self, set_, q):
            first, self.depth = SETS[set_][0][q], SETS[set_][1]
            self.order = LINKS[first:] + LINKS[:first]
            self.set, self.q, self.stage, self.n = set_, q, -1, 64
            self.key = "%s%d_" % (set_, q)
            self.cur = r[self.key + "buf"]
            self.weight = {bit: 32 >> k for k, bit in enumerate(self.order)}

        def index(self, **bits):
            return sum(value * self.weight[bit] for bit, value in bits.items())

        def begin(self):
            self.stage += 1
            k, n = self.stage, self.n
            if k < 6:
                self.into = r[self.key + "in%d" % k]
                self.copies = [remote(self.cur.at[pl.ds(n // 2, n // 2)], self.into, partner[self.order[k]])]
                return
            count = len(SETS[self.set][0])
            dst = r["out_" + self.set].at[
                pl.ds(pl.multiple_of(l * self.depth, self.depth), self.depth),
                pl.ds(pl.multiple_of((count * c + self.q) * 256, LANES), 256),
            ]
            self.copies = [remote(self.cur.at[0], dst, partner[way]) for way in ("L", "C", "D")]
            self.copy_here = here(self.cur.at[0], dst)

        def finish(self):
            for copy in self.copies:
                copy.wait_recv()
            if self.stage == 6:
                self.copy_here.wait()
                return
            self.n //= 2
            cur, into = self.cur, self.into
            m = min(self.n, 4)

            def step(i):
                rows = pl.ds(i * m, m)
                cur[rows] = (cur[rows].astype(F32) + into[rows].astype(F32)).astype(B16)

            if self.n > m:
                loop(self.n // m, step)
            else:
                step(0)

        def advance(self):
            self.finish()
            if self.stage < 6:
                self.begin()

    parts = {(set_, q): Part(set_, q) for set_ in SETS for q in range(len(SETS[set_][0]))}

    def advance(set_, *some):
        for q in some or range(len(SETS[set_][0])):
            parts[set_, q].advance()

    def product(x_ref, y_ref, width, pieces, add=False):
        span = 512 if width <= 512 else 256
        per = span // 256

        def step(i):
            columns = block(i, span)
            whole = tdot(x_ref[:, columns], y_ref[...])
            for a in range(per):
                zz = i * per + a
                zb = lax.rem(lax.div(z, 2) + lax.div(zz, 2), 2)
                za = lax.rem(lax.rem(z, 2) + lax.rem(zz, 2) + zb, 2)
                for xx in range(4):
                    xb = lax.rem(lax.div(x, 2) + xx // 2, 2)
                    xa = lax.rem(lax.rem(x, 2) + xx % 2 + xb, 2)
                    at = (a * 4 + xx) * 64
                    for part, src, width_, half in pieces:
                        for k in range(64 // part.depth):
                            ll = k % 2
                            o = half if half is not None else lax.rem(k // 2 + t, 2)
                            idx = part.index(ZA=za, ZB=zb, XA=xa, XB=xb, O=o, L=lax.rem(ll + l + o, 2))
                            value = whole[at + k * part.depth : at + (k + 1) * part.depth, src : src + width_]
                            to = pl.ds(0, width_)
                            if add:
                                value = value + part.cur[idx, :, to].astype(F32)
                            part.cur[idx, :, to] = value.astype(B16)

        loop(WIDE // span, step)

    def heads(q, at=0):
        return [("S", q, at, 0), ("S", q, at + 256, 1)]

    def product_heads(x_ref, y_ref, width, wanted):
        product(x_ref, y_ref, width, [(parts["S", q], at, 256, half) for _, q, at, half in wanted])

    def product_rows(x_ref, y_ref, width, set_, q, add=False):
        pieces, at = [], 0
        while at < width:
            n = min(256, width - at)
            pieces.append((parts[set_, q + at // 256], at, n, None))
            at += n
        product(x_ref, y_ref, width, pieces, add)

    r["gains"][...] = jnp.zeros_like(r["gains"])

    def norm_grad(value_ref, gain, slot, after):
        def step(i):
            rows = block(i, 64)
            high, inverse = norm_parts(value_ref[rows, :].astype(F32))
            e = r["v_tmp"][rows, :]
            a = e * gain
            back = (
                a - jnp.mean(a, axis=-1, keepdims=True) - high * jnp.mean(a * high, axis=-1, keepdims=True)
            ) * inverse
            r["gains"][pl.ds(slot, 1), :] += jnp.sum(e * high, axis=0, keepdims=True)
            after(rows, back)

        loop(ROWS // 64, step)

    def add_grad(low_ref):
        def after(rows, back):
            total = r["v_grad"][rows, :] + back
            r["v_grad"][rows, :] = total
            low_ref[rows, :] = total.astype(B16)

        return after

    def pull(a_ref, w_ref, store):
        def step(i):
            rows = block(i, 256)
            store(rows, dot_t(a_ref[...], w_ref[rows, :]))

        loop(w_ref.shape[0] // 256, step)

    def to_tmp(columns, value):
        r["v_tmp"][:, columns] = value

    def halves(name, src, to):
        copy = remote(src.at[:, give512], to.at[low], sib)
        ready[name] = [here(src.at[:, keep512], to.at[top]).wait, copy.wait_recv]
        return copy

    await_all("after_attend")

    def feed_norm(i):
        rows = block(i, 64)
        high, _ = norm_parts(r["v_norm"][rows, :])
        x2[rows, :] = (high * r["norm_gains"][3:4, :]).astype(B16)

    loop(ROWS // 64, feed_norm)
    feed_in_copy = remote(x2.at[top], x2.at[low], sib)
    await_all("up", "cot", "down")

    def feed_step(i):
        columns = block(i, 256)
        hidden = dot(x2[top, :], up_w[:, columns])
        r["v_feed_act"][:, columns] = gelu(hidden).astype(B16)
        pulled = dot_t(x1[top, :], down_w[columns, :])
        r["v_feed_back"][:, columns] = (gelu_slope(hidden) * pulled).astype(B16)

    loop(4, feed_step)
    quarter_sends = []
    for name in ("feed_act", "feed_back"):
        ref, to = r["v_" + name], r["y_" + name]
        quarter_sends += [
            remote(ref.at[:, give256], to.at[low, left], sib),
            remote(ref.at[:, pl.ds(768, 256)], to.at[low, right], sib),
        ]
        ready["y_" + name] = [
            here(ref.at[:, keep256], to.at[top, left]).wait,
            here(ref.at[:, pl.ds(512, 256)], to.at[top, right]).wait,
        ] + [copy.wait_recv for copy in quarter_sends[-2:]]
    pull(r["v_feed_back"], up_w, to_tmp)

    def feed_after(rows, back):
        total = x1[rows, :].astype(F32) + back
        r["v_grad"][rows, :] = total
        x3[rows, :] = total.astype(B16)

    norm_grad(r["v_norm"], r["norm_gains"][3:4, :], 3, feed_after)
    branch_copy = remote(x3.at[top], x3.at[low], sib)
    load("cross_up", up_w, "cross_up")

    def latents_step(i):
        columns = block(i, 256)
        r["v_latents_out"][:, columns] = (
            r["v_norm"][:, columns] + dot(r["v_feed_act"][...], down_w[:, columns])
        ).astype(B16)

    loop(4, latents_step)
    load("cross_down", down_w, "cross_down")
    load("after_mlp", r["v_norm"], "after_mlp")
    out_move, out_stay = remote_of(r["v_latents_out"], r["latents_home"], peer(0)), here_of(r["v_latents_out"], r["latents_home"])

    @pl.when(c != t)
    def _():
        out_move.start()

    @pl.when(c == t)
    def _():
        out_stay.start()

    await_all("y_feed_act")
    product_heads(x1, r["y_feed_act"], 512, heads(0))
    parts["S", 0].begin()
    load("cross_act", x1, "x_cross_act")
    feed_in_copy.wait_recv()
    await_all("y_feed_back")
    product_heads(x2, r["y_feed_back"], 512, heads(1))
    parts["S", 1].begin()
    sent(feed_in_copy)
    load("late_x", x2, "x_late_x")

    branch_copy.wait_recv()
    await_all("out_mine", "projected", "probs", "mixed")

    def mixed_step(columns, value):
        r["v_self_grad"][:, columns] = value.astype(B16)

    pull(x3, r["w_out_mine"], mixed_step)
    product_heads(x3, r["y_mixed"], 512, heads(2))
    parts["S", 2].begin()
    sent(branch_copy)
    load("cross_in", x3, "x_cross_in")
    projected, y_back = r["v_projected"], r["y_back"]

    def attend_back(h):
        columns = block(h, HEAD_WIDTH)
        query, key, value = (projected[k, :, columns] for k in range(3))
        key_sum = value_sum = 0
        for j in range(2):
            rows = pl.ds(ROWS * j, ROWS)
            grad = r["v_self_grad"][rows, columns]
            p = probs[2 * h + j]
            g = dot_t(grad, value)
            p32 = p.astype(F32)
            change = (p32 * (g - jnp.sum(p32 * g, axis=-1, keepdims=True))).astype(B16)
            y_back[rows, columns] = (dot(change, key) * self_scale).astype(B16)
            key_sum = key_sum + tdot(change, projected[0, rows, columns])
            value_sum = value_sum + tdot(p, grad)
        y_back[:, pl.ds(pl.multiple_of(512 + h * HEAD_WIDTH, LANES), HEAD_WIDTH)] = (key_sum * self_scale).astype(B16)
        y_back[:, pl.ds(pl.multiple_of(1024 + h * HEAD_WIDTH, LANES), HEAD_WIDTH)] = value_sum.astype(B16)

    loop(4, attend_back)
    load("raised", probs)
    await_all("attend_own", "attend_far")

    def rows_step(i):
        rows = block(i, 256)
        total = 0
        for k in range(3):
            total = total + dot_t(y_back[:, pl.ds(512 * k, 256)], r["w_attend_own"][k, rows, :])
            total = total + dot_t(y_back[:, pl.ds(512 * k + 256, 256)], r["w_attend_far"][k, rows, :])
        r["v_tmp"][:, rows] = total[:ROWS]
        r["v_rows_give"][:, rows] = total[ROWS:].astype(B16)

    loop(4, rows_step)
    rows_copy = remote(r["v_rows_give"], r["v_rows_in"], sib)
    await_all("attend_in")
    product_heads(x4, y_back, 1536, [piece for k in range(3) for piece in heads(3 + k, 512 * k)])
    for q in (3, 4, 5):
        parts["S", q].begin()
    load("attended", x4, "x_attended")
    rows_copy.wait_recv()

    def sum_step(i):
        rows = block(i, 64)
        r["v_tmp"][rows, :] += r["v_rows_in"][rows, :].astype(F32)

    loop(ROWS // 64, sum_step)
    await_all("after_mlp")
    mlp_branch, cross_branch = r["v_branch"], r["v_rows_give"]
    norm_grad(r["v_norm"], r["norm_gains"][2:3, :], 2, add_grad(mlp_branch))
    load("after_cross", r["v_norm"], "after_cross")

    halves("y_mlp", mlp_branch, r["y_mlp"])
    await_all("cross_down", "cross_hidden")

    def hidden_store(columns, value):
        r["v_back"][:, columns] = (gelu_slope(r["v_hidden"][:, columns]) * value).astype(B16)

    pull(mlp_branch, down_w, hidden_store)
    load("cross_out", down_w, "cross_out")
    halves("y_hidden", r["v_back"], r["y_hidden"])
    await_all("cross_up")
    pull(r["v_back"], up_w, to_tmp)
    load("query_weight", up_w, "query_weight")
    advance("S", 0, 1)
    sent(rows_copy)
    await_all("after_cross")
    norm_grad(r["v_norm"], r["norm_gains"][1:2, :], 1, add_grad(cross_branch))
    halves("y_out", cross_branch, r["y_out"])
    await_all("cross_out")

    def attended_store(columns, value):
        x5[top, columns] = value.astype(B16)

    pull(cross_branch, down_w, attended_store)
    attended_copy = remote(x5.at[top], x5.at[low], sib)
    await_all("x_cross_act", "y_mlp")
    product_rows(x1, r["y_mlp"], 512, "P", 0)
    parts["P", 0].begin()
    parts["P", 1].begin()
    await_all("x_cross_in", "y_hidden")
    product_rows(x3, r["y_hidden"], 512, "P", 2)
    parts["P", 2].begin()
    parts["P", 3].begin()
    advance("S", 2)

    await_all("value_wide", "mixed_f32", "asked", "picture", "raised")
    pull_low = dot_t(x5[top, :], r["w_value"][...]).astype(B16)
    r["v_pull"][...] = pull_low
    pull_f32 = pull_low.astype(F32)
    r["v_dot"][...] = jnp.sum(pull_f32 * r["v_mixed"][...], axis=-1, keepdims=True)
    scale_any = r["inverse_total"][...] * r["any_kept"][...]
    r["v_asked_t"][...] = (r["v_asked"][...].astype(F32) * scale_any).T.astype(B16)
    r["v_pull_t"][...] = (pull_f32 * r["inverse_total"][...]).T.astype(B16)
    r["v_sum"][...] = jnp.zeros_like(r["v_sum"])

    def pixel_chunk(i, to, at):
        picture, raised = r["v_picture"][:, block(i, 512)], probs[i]
        change = (raised.astype(F32) * (dot(r["v_pull"][...], picture) - r["v_dot"][...])).astype(B16)
        r["v_sum"][...] += dot_t(change, picture)
        to[:, block(at, 512)] = (dot(r["v_asked_t"][...], change) + dot(r["v_pull_t"][...], raised)).astype(B16)

    loop(4, lambda i: pixel_chunk((1 - c) * 4 + i, r["grad_far"], i))
    grad_copy = remote(r["grad_far"], r["grad_in"], sib)
    loop(4, lambda i: pixel_chunk(c * 4 + i, r["grad_own"], i))

    turned_sum = r["v_sum"][...] * scale_any
    r["y_late_own"][...] = jnp.zeros_like(r["y_late_own"])
    r["y_late_own"][:, :PAD] = (turned_sum * cross_scale).astype(B16)
    ready["y_late"] = [
        here(r["y_late_own"], r["y_late"].at[top]).wait,
        remote(r["y_late_own"], r["y_late"].at[low], sib).wait_recv,
    ]
    r["gains"][4:5, :PAD] = jnp.sum(
        r["v_asked"][...].astype(F32) * turned_sum + pull_f32 * r["v_mixed"][...], axis=0, keepdims=True
    )

    grad_copy.wait_recv()

    def grad_step(i):
        rows = block(i, 16)
        r["grad_own"][rows, :] = (r["grad_own"][rows, :].astype(F32) + r["grad_in"][rows, :].astype(F32)).astype(B16)

    loop(PAD // 16, grad_step)

    def homeward_of(k):
        to = lax.rem(s + k, seq)
        return remote_of(r["grad_own"].at[:, block(to, LANES)], r["home"].at[s], peer(k))

    homeward = [homeward_of(k) for k in range(seq)]
    stay = here_of(r["grad_own"].at[:, block(s, LANES)], r["home"].at[s])

    @pl.when(c != t)
    def _():
        homeward[0].start()

    @pl.when(c == t)
    def _():
        stay.start()

    for k in range(1, seq):
        homeward[k].start()

    await_all("x_attended", "y_out")
    product_rows(x4, r["y_out"], 512, "Q", 0)
    parts["Q", 0].begin()
    parts["Q", 1].begin()
    attended_copy.wait_recv()
    await_all("mixed_pixels")
    product_rows(x5, r["y_mixed_pixels"], 512, "Q", 2)
    await_all("x_late_x", "y_late")
    product_rows(x2, r["y_late"], 384, "Q", 2, add=True)
    parts["Q", 2].begin()
    parts["Q", 3].begin()
    advance("S", 3, 4, 5)
    advance("S", 0, 1, 2)
    advance("P")

    sent(*quarter_sends)
    latents, latgrad = r["v_feed_act"], r["v_feed_back"]
    load("latents_turned", latents)
    await_all("key_wide", "query_weight", "latents_turned")
    r["v_rows_in"][...] = dot(r["y_late_own"][:, :PAD], r["w_key"][...]).astype(B16)
    pull(r["v_rows_in"], up_w, to_tmp)

    def latents_after(rows, back):
        latgrad[rows, :] = (r["v_grad"][rows, :] + back).astype(B16)

    norm_grad(latents, r["norm_gains"][0:1, :], 0, latents_after)
    grad_move, grad_stay = remote_of(latgrad, r["latgrad_home"], peer(0)), here_of(latgrad, r["latgrad_home"])

    @pl.when(c != t)
    def _():
        grad_move.start()

    @pl.when(c == t)
    def _():
        grad_stay.start()

    gain_buf, gain_in = r["gain_buf"], r["gain_in"]
    gain_buf[0] = r["gains"][...]
    gain_steps = LINKS + ("C",)
    gain_copy = remote(gain_buf.at[0], gain_in.at[0], partner[gain_steps[0]])
    live = [parts[key] for key in parts]
    k = 0
    while live or k < 7:
        if k < 7:
            gain_copy.wait_recv()
            total = gain_buf[k] + gain_in[k]
            k += 1
            if k < 7:
                gain_buf[k] = total
                gain_copy = remote(gain_buf.at[k], gain_in.at[k], partner[gain_steps[k]])
            else:
                r["out_gains"][...] = total
        left_over = []
        for part in live:
            last = part.stage == 6
            part.advance()
            if not last:
                left_over.append(part)
        live = left_over

    @pl.when(c != t)
    def _():
        out_move.wait()
        grad_move.wait()
        homeward[0].wait()

    @pl.when(c == t)
    def _():
        out_stay.wait()
        grad_stay.wait()
        stay.wait()

    for k in range(1, seq):
        homeward[k].wait()
    for copy in waits:
        copy.wait_send()
    assert not ready, tuple(ready)
    assert used[0] <= sems[0] and used[1] <= sems[1], used


def back_and_reduce(given):
    names, scratch = [], []

    def room(name, shape, dtype=B16):
        names.append(name)
        scratch.append(pltpu.VMEM(shape, dtype))

    sems = (200, 96)
    names += list(BACK_HBM) + list(BACK_VMEM) + list(BACK_OUT)
    for name in ("send", "recv", "local"):
        names.append(name)
        scratch.append(pltpu.SemaphoreType.DMA((sems[1 if name == "local" else 0],)))
    for k in range(1, 6):
        room("x%d" % k, (512, WIDE))
    for name in ("feed_act", "feed_back", "mixed", "mixed_pixels", "mlp", "hidden", "out"):
        room("y_" + name, (512, 512))
    room("y_back", (512, 1536))
    room("y_late", (512, 384))
    room("y_late_own", (ROWS, 384))
    for name in ("w_down", "w_up"):
        room(name, (WIDE, WIDE))
    room("w_out_mine", (512, WIDE))
    for name in ("w_attend_own", "w_attend_far"):
        room(name, (3, WIDE, 256))
    for name in ("w_key", "w_value"):
        room(name, (PAD, WIDE))
    for name in ("v_tmp", "v_norm", "v_grad", "v_hidden"):
        room(name, (ROWS, WIDE), F32)
    for name in ("rows_in", "rows_give", "branch", "back", "feed_act", "feed_back", "latents_out"):
        room("v_" + name, (ROWS, WIDE))
    room("v_projected", (3, 512, 512))
    room("v_probs", (8, ROWS, 512))
    room("v_self_grad", (512, 512))
    room("v_picture", (PAD, 4096))
    room("v_mixed", (ROWS, PAD), F32)
    room("v_sum", (ROWS, PAD), F32)
    room("v_asked", (ROWS, PAD))
    room("v_pull", (ROWS, PAD))
    room("v_asked_t", (PAD, ROWS))
    room("v_pull_t", (PAD, ROWS))
    room("v_dot", (ROWS, 1), F32)
    for name in ("grad_own", "grad_far", "grad_in"):
        room(name, (PAD, 16 * LANES))
    room("gains", (8, WIDE), F32)
    room("gain_buf", (7, 8, WIDE), F32)
    room("gain_in", (7, 8, WIDE), F32)
    for set_, (firsts, depth) in SETS.items():
        for q in range(len(firsts)):
            key = "%s%d_" % (set_, q)
            room(key + "buf", (64, depth, 256))
            for k in range(6):
                room(key + "in%d" % k, (32 >> k, depth, 256))
    anywhere = pl.BlockSpec(memory_space=pl.ANY)
    vmem = pl.BlockSpec(memory_space=pltpu.VMEM)
    result = pl.pallas_call(
        functools.partial(back_kernel, tuple(names), sems),
        out_shape=[jax.ShapeDtypeStruct(*spec) for spec in BACK_OUT.values()],
        in_specs=[anywhere] * len(BACK_HBM) + [vmem] * len(BACK_VMEM),
        out_specs=[anywhere] * (len(BACK_OUT) - 1) + [vmem],
        scratch_shapes=scratch,
        compiler_params=pltpu.CompilerParams(collective_id=1, has_side_effects=True, vmem_limit_bytes=63 * MIB),
        name="back_and_reduce",
    )(*[given[name] for name in BACK_HBM + BACK_VMEM])
    return dict(zip(BACK_OUT, result))


FINISH_IN = ("pixels", "home", "out_S", "out_P", "out_Q", "latgrad_home", "latents_home", "key_wide")
FINISH_OUT = ("pixels_grad", "latents_grad", "latents_out")


def finish_kernel(*refs):
    refs = list(refs)

    def take(n):
        part = refs[:n]
        del refs[:n]
        return part

    hbm = dict(zip(FINISH_IN, take(len(FINISH_IN))))
    gain, gains = take(2)
    results = dict(zip(FINISH_OUT, take(len(FINISH_OUT))))
    gain_rows, pixelgain, query_grad, key_grad, value_grad, crossout, crossup, crossdown = take(8)
    selfattend, selfout, selfup, selfdown = take(4)
    vmem = dict(zip(FINISH_IN, take(len(FINISH_IN))))
    turned, high, grad, latgrad, sems = take(5)
    pixels, home = vmem["pixels"], vmem["home"]
    channels = pixels.shape[0]

    copies = {
        name: pltpu.make_async_copy(hbm[name], vmem[name], sems.at[k])
        for k, name in enumerate(FINISH_IN)
    }
    last = len(FINISH_IN)
    straight = pltpu.make_async_copy(vmem["latents_home"], results["latents_out"], sems.at[last])
    for copy in copies.values():
        copy.start()

    some = 9

    def features(i):
        return pl.ds(i * some, some)

    steps = channels // some
    copies["pixels"].wait()
    zeros = jnp.zeros(pixels.shape[1:], F32)
    average = lax.fori_loop(
        0, steps, lambda i, total: total + jnp.sum(pixels[features(i)].astype(F32), axis=0), zeros
    ) * (1.0 / channels)

    def square_step(i, total):
        centered = pixels[features(i)].astype(F32) - average
        return total + jnp.sum(centered * centered, axis=0)

    inverse = lax.rsqrt(lax.fori_loop(0, steps, square_step, zeros) * (1.0 / channels) + EPS)
    copies["home"].wait()
    for image in range(16):
        turned[pl.ds(image, PAD, stride=16), :] = home[image].astype(F32)

    def mean_step(i, totals):
        h = (pixels[features(i)].astype(F32) - average) * inverse
        rows = pl.ds(pl.multiple_of(i * (some * 16), 16), some * 16)
        a = turned[rows, :].reshape(some, 16, LANES) * gain[features(i)]
        high[features(i)] = h
        grad[features(i)] = a
        return totals[0] + jnp.sum(a, axis=0), totals[1] + jnp.sum(a * h, axis=0)

    first, second = lax.fori_loop(0, steps, mean_step, (zeros, zeros))
    first, second = first * (1.0 / channels), second * (1.0 / channels)

    def grad_step(i):
        grad[features(i)] = (grad[features(i)] - first - high[features(i)] * second) * inverse

    loop(steps, grad_step)
    pixels_out = pltpu.make_async_copy(grad, results["pixels_grad"], sems.at[last + 1])
    pixels_out.start()
    copies["latents_home"].wait()
    straight.start()
    copies["latgrad_home"].wait()
    latgrad[...] = vmem["latgrad_home"][...].astype(F32)
    latents_out = pltpu.make_async_copy(latgrad, results["latents_grad"], sems.at[last + 2])
    latents_out.start()

    for name in ("out_S", "out_P", "out_Q", "key_wide"):
        copies[name].wait()
    out_s, out_p, out_q = vmem["out_S"], vmem["out_P"], vmem["out_Q"]
    late = [out_q[:, 512:1024], out_q[:, 1536:2048]]
    query_grad[...] = dot(late[0][:, :PAD], vmem["key_wide"][...])
    key_grad[...] = late[1][:, :channels].astype(F32)
    value_grad[:, :LANES] = late[0][:, 384:].astype(F32)
    value_grad[:, LANES : 2 * LANES] = late[1][:, 384:].astype(F32)
    value_grad[:, 2 * LANES :] = late[0][:, 256:384].astype(F32)[:, 16 : 16 + channels - 2 * LANES]
    for k, ref in enumerate((crossdown, crossup)):
        for core in range(2):
            ref[:, pl.ds(512 * core, 512)] = out_p[:, pl.ds(1024 * core + 512 * k, 512)].astype(F32)
    for core in range(2):
        crossout[:, pl.ds(512 * core, 512)] = out_q[:, pl.ds(1024 * core, 512)].astype(F32)

    def item(k, core):
        return out_s[:, pl.ds(1536 * core + 256 * k, 256)].astype(F32)

    for core in range(2):
        columns = pl.ds(256 * core, 256)
        selfdown[:, columns] = item(0, core)
        selfup[:, columns] = item(1, core)
        selfout[:, columns] = item(2, core)
        for k in range(3):
            selfattend[k, :, columns] = item(3 + k, core)

    mine = 2 * lax.axis_index("seq") + lax.axis_index("tensor")
    rolled = pltpu.roll(gains[...], lax.rem(WIDE - 32 * mine, WIDE), 1)
    for k, ref in enumerate(gain_rows_of(gain_rows)):
        ref[...] = rolled[k : k + 1, :32]
    pixelgain[...] = gains[4:5, :channels]
    straight.wait()
    pixels_out.wait()
    latents_out.wait()


def gain_rows_of(ref):
    return [ref.at[pl.ds(k, 1)] for k in range(4)]


def finish(given):
    pixels = given["pixels"]
    channels, images, rows = pixels.shape
    small = [
        (4, 32),
        (1, channels),
        (32, WIDE),
        (32, channels),
        (32, channels),
        (32, WIDE),
        (32, WIDE),
        (32, WIDE),
        (3, 64, 512),
        (64, 512),
        (64, 512),
        (64, 512),
    ]
    anywhere = pl.BlockSpec(memory_space=pl.ANY)
    vmem = pl.BlockSpec(memory_space=pltpu.VMEM)
    return pl.pallas_call(
        finish_kernel,
        out_shape=[
            jax.ShapeDtypeStruct(pixels.shape, F32),
            jax.ShapeDtypeStruct((ROWS, WIDE), F32),
            jax.ShapeDtypeStruct((ROWS, WIDE), B16),
        ]
        + [jax.ShapeDtypeStruct(shape, F32) for shape in small],
        in_specs=[anywhere] * len(FINISH_IN) + [vmem] * 2,
        out_specs=[anywhere] * 3 + [vmem] * len(small),
        scratch_shapes=[pltpu.VMEM(given[name].shape, given[name].dtype) for name in FINISH_IN]
        + [
            pltpu.VMEM((PAD * images, rows), F32),
            pltpu.VMEM(pixels.shape, F32),
            pltpu.VMEM(pixels.shape, F32),
            pltpu.VMEM((ROWS, WIDE), F32),
            pltpu.SemaphoreType.DMA((len(FINISH_IN) + 3,)),
        ],
        compiler_params=pltpu.CompilerParams(vmem_limit_bytes=60 * MIB),
        name="finish",
    )(*[given[name] for name in FINISH_IN], given["pixel_gain"], given["out_gains"])


def shards(
    latents,
    pixels,
    crop_bounds,
    key_mask,
    query_gain,
    pixel_gain,
    cross_gain,
    attend_gain,
    feed_gain,
    query_weight,
    key_weight,
    value_weight,
    cross_out,
    cross_up,
    cross_down,
    self_attend,
    self_out,
    self_up,
    self_down,
    cotangent,
):
    channels = pixels.shape[2]
    given = {
        "pixels": jnp.transpose(pixels, (2, 0, 1)),
        "latents": latents[0],
        "cotangent": cotangent[0],
        "query_weight": query_weight,
        "key_weight": key_weight,
        "value_weight": value_weight,
        "cross_out": cross_out,
        "cross_up": cross_up,
        "cross_down": cross_down,
        "self_attend": self_attend,
        "self_out": self_out,
        "self_up": self_up,
        "self_down": self_down,
        "norm_gains": jnp.stack([query_gain, cross_gain, attend_gain, feed_gain]).astype(F32),
        "pixel_gain": jnp.broadcast_to(pixel_gain.astype(F32)[:, None, None], (channels, 1, LANES)),
        "key_mask": key_mask,
        "crop_bounds": crop_bounds,
    }
    given |= front(given)
    given |= back_and_reduce(given)
    (
        pixels_grad,
        latents_grad,
        latents_out,
        gain_rows,
        pixelgain,
        queryweight_grad,
        keyweight_grad,
        valueweight_grad,
        crossout_grad,
        crossup_grad,
        crossdown_grad,
        selfattend_grad,
        selfout_grad,
        selfup_grad,
        selfdown_grad,
    ) = finish(given)
    return (
        latents_out[None],
        latents_grad[None],
        jnp.transpose(pixels_grad, (1, 2, 0)),
        gain_rows[0],
        pixelgain[0] / pixel_gain.astype(F32),
        gain_rows[1],
        gain_rows[2],
        gain_rows[3],
        queryweight_grad,
        keyweight_grad.T,
        valueweight_grad.T,
        crossout_grad,
        crossup_grad,
        crossdown_grad,
        selfattend_grad,
        selfout_grad.T,
        selfup_grad,
        selfdown_grad.T,
    )


def solution(mesh):
    in_specs = (
        P(("batch", "seq"), "tensor", None),
        P("batch", ("seq", "tensor"), None),
        P(("batch", "seq"), None),
        P(("batch", "seq"), None),
        P(),
        P(),
        P(),
        P(),
        P(),
        P(),
        P(),
        P(),
        P(),
        P(),
        P(),
        P(None, None, "tensor"),
        P("tensor", None),
        P(None, "tensor"),
        P("tensor", None),
        P(("batch", "seq"), "tensor", None),
    )
    out_specs = (
        P(("batch", "seq"), "tensor", None),
        P(("batch", "seq"), "tensor", None),
        P("batch", ("seq", "tensor"), None),
        P(("seq", "tensor")),
        P(),
        P(("seq", "tensor")),
        P(("seq", "tensor")),
        P(("seq", "tensor")),
        P(("seq", "tensor"), None),
        P(None, ("seq", "tensor")),
        P(None, ("seq", "tensor")),
        P(("seq", "tensor"), None),
        P(("seq", "tensor"), None),
        P(("seq", "tensor"), None),
        P(None, "seq", "tensor"),
        P("tensor", "seq"),
        P("seq", "tensor"),
        P("tensor", "seq"),
    )
    return jax.shard_map(shards, mesh=mesh, in_specs=in_specs, out_specs=out_specs, check_vma=False)
```

time: 248 us -> 208 us (0.84)
  Pallas kernels: 214 us -> 199 us
  other arithmetic: 13.1 us -> 1.92 us
  local copies, waits for them, and re-layouts: 16.8 us -> 5.77 us
    pallas_call x1, Pallas kernels: 98.8 us -> 80 us  [front(): pl.pallas_call(functools.partial(front_kernel, tuple(names), sems), out_s...]
    pallas_call x0 -> x1, Pallas kernels: none -> 8.29 us  [finish(): pl.pallas_call(finish_kernel, out_shape=[jax.ShapeDtypeStruct(pixels.shap...]
    unnamed x41 -> x2, local copies, waits for them, and re-layouts: 6.64 us -> 0.01 us
    pallas_call x1, Pallas kernels: 115 us -> 110 us  [back_and_reduce(): pl.pallas_call(functools.partial(back_kernel, tuple(names), sems), out_sh...]
    reduce_sum x3 -> x0, other arithmetic: 3.82 us -> none  [the longest x1 1.57 us: norm_parts(): spread = jnp.mean(centered * centered, axis=-1, keepdims=True)]
    broadcast_in_dim x5 -> x0, other arithmetic: 3.46 us -> none  [the longest x1 1.08 us: shards(): latents_grad.astype(F32)[None]]
    slice x7 -> x0, local copies, waits for them, and re-layouts: 2.77 us -> none  [the longest x1 1.06 us: shards(): heads_sums = [out_s[:, :, k].reshape(64, 512).astype(F32) for k in range(6)]]
    pad x4 -> x0, local copies, waits for them, and re-layouts: 2.76 us -> none  [the longest x1 1.07 us: shards(): jnp.pad(jnp.swapaxes(pixel_low, 1, 2), ((0, 0), (0, PAD - channels), (0,...]
where the time goes in v1:
time: 208 us; the launch traced here: 207 us
  Pallas kernels  199 us (96%)
  local copies, waits for them, and re-layouts  5.77 us (3%)
    pallas_call x1, Pallas kernels, back_and_reduce(): pl.pallas_call(functools.partial(back_kernel, tuple(names), sems), out_sh...  110 us
    pallas_call x1, Pallas kernels, front(): pl.pallas_call(functools.partial(front_kernel, tuple(names), sems), out_s...  80 us
    pallas_call x1, Pallas kernels, finish(): pl.pallas_call(finish_kernel, out_shape=[jax.ShapeDtypeStruct(pixels.shap...  8.29 us

profile of v1, /device:TPU:1, one launch (start us, length us, event | category | flops | bytes accessed | tf_op | source)
XLA Modules:
  0.0 207.1 jit_solution(14055101069885377866)
XLA Ops:
  0.7 0.7 stack.15
  1.3 0.7 stack.16
  2.0 0.7 stack.17
  2.7 0.7 stack.18
  3.4 0.6 maximum_convert_fusion.refs_11_.refs_34_
  4.0 1.7 broadcast_in_dim.12.refs_12_.refs_8_
  5.7 80.0 %front.1 = (bf16[512,1024]{1,0:T(8,128)(2,1)}, bf16[512,1024]{1,0:T(8,128)(2,1)}, bf16[512,1024]{1,0:T(8,128)(2,1)}, bf16[512,1024]{1,0:T(8,128)(2,1)}, bf16[512...) custom-call(bf16[261,16,128]{2,1,0:T(8,128)(2,1)} %bitcast.18, ...), custom_call_target="tpu_custom_call" | custom-call | tf_op jit(solution)/shard_map/front/pallas_call | solution.py:642
  85.7 110.4 %back_and_reduce.1 = (bf16[64,3072]{1,0:T(8,128)(2,1)}, bf16[32,2048]{1,0:T(8,128)(2,1)}, bf16[32,2048]{1,0:T(8,128)(2,1)}, bf16[16,272,128]{2,1,0:T(8,128)(2,1)...) custom-call(bf16[512,1024]{1,0:T(8,128)(2,1)} %get-tuple-element.67.refs_0_, ...), custom_call_target="tpu_custom_call" | custom-call | tf_op jit(solution)/shard_map/back_and_reduce/pallas_call | solution.py:1286
  196.2 0.0 copy-start
  196.2 8.3 %finish.1 = (f32[261,16,128]{2,1,0:T(8,128)}, f32[256,1024]{1,0:T(8,128)}, bf16[256,1024]{1,0:T(8,128)(2,1)}, f32[4,32]{1,0:T(4,128)}, f32[1,261]{1,0:T(1,128)},...) custom-call(bf16[261,16,128]{2,1,0:T(8,128)(2,1)} %bitcast.19, ...), custom_call_target="tpu_custom_call" | custom-call | tf_op jit(solution)/shard_map/finish/pallas_call | solution.py:1433
  204.5 0.7 reduce
  205.2 0.0 copy-done
  205.2 0.6 convert_divide_fusion
  205.8 1.3 slice_bitcast_fusion
Async XLA Ops:
  196.2 9.0 %copy-start = (bf16[261]{0:T(512)(128)(2,1)S(1)}, bf16[261]{0:T(512)(128)(2,1)}, u32[]{:S(2)}) copy-start(bf16[261]{0:T(512)(128)(2,1)} %param.25) | copy-start | bytes 1570

commit v2 on v1

--- a/solution.py
+++ b/solution.py
@@ -66,6 +66,16 @@
     lax.fori_loop(0, n, lambda i, carry: (step(i), carry)[1], 0)
 
 
+def row_of(ref):
+    return ref[...].astype(F32).reshape(1, ref.shape[0])
+
+
+def per_feature(gain_ref, out_ref):
+    channels = gain_ref.shape[0]
+    wide = jnp.concatenate([row_of(gain_ref), jnp.zeros((1, 384 - channels), F32)], axis=1)
+    out_ref[...] = jnp.broadcast_to(wide, (LANES, 384)).T
+
+
 def block(i, n):
     return pl.ds(pl.multiple_of(i * n, n), n)
 
@@ -74,7 +84,7 @@
     ("pixels", "latents", "cotangent", "self_attend", "self_out", "self_up", "self_down")
     + ("query_weight", "cross_out", "cross_up", "cross_down")
 )
-FRONT_VMEM = ("norm_gains", "pixel_gain", "key_weight", "value_weight", "key_mask", "crop_bounds")
+FRONT_VMEM = ("query_gain", "cross_gain", "attend_gain", "feed_gain", "pixel_gain", "key_weight", "value_weight", "key_mask", "crop_bounds")
 FRONT_OUT = {
     "cot": ((512, WIDE), B16),
     "cross_act": ((512, WIDE), B16),
@@ -103,8 +113,9 @@
     "value_wide": ((PAD, WIDE), B16),
     "inverse_total": ((ROWS, 1), F32),
     "any_kept": ((1, 1), F32),
+    "norm_gains": ((8, WIDE), F32),
 }
-FRONT_OUT_VMEM = ("inverse_total", "any_kept")
+FRONT_OUT_VMEM = ("inverse_total", "any_kept", "norm_gains")
 
 
 def front_kernel(names, sems, *refs):
@@ -116,13 +127,12 @@
     self_scale = 1.0 / math.sqrt(HEAD_WIDTH)
     sib = (2 * l + 1 - c, s, t)
     over = (2 * (1 - l) + c, s, 1 - t)
-    beside = (2 * (1 - l) + c, s, t)
 
     def peer(k):
         return (2 * l + t, lax.rem(s + k, seq), c)
 
     barrier = pltpu.get_barrier_semaphore()
-    for device in (sib, over, beside):
+    for device in (sib, over):
         pl.semaphore_signal(barrier, inc=1, device_id=device, device_id_type=MESH)
     def plane(k):
         return (2 * l + c, lax.rem(s + k, seq), t)
@@ -134,11 +144,11 @@
     @pl.when(c != t)
     def _():
         pl.semaphore_signal(barrier, inc=1, device_id=peer(0), device_id_type=MESH)
-        pl.semaphore_wait(barrier, 2 + 2 * seq)
+        pl.semaphore_wait(barrier, 1 + 2 * seq)
 
     @pl.when(c == t)
     def _():
-        pl.semaphore_wait(barrier, 1 + 2 * seq)
+        pl.semaphore_wait(barrier, 2 * seq)
 
     used = [0, 0]
     waits, stores = [], []
@@ -195,24 +205,14 @@
         )
 
     away = [away_of(k) for k in range(seq)]
-    lat_move, cot_move = remote_of(r["latents"], r["v_lat"], peer(0)), remote_of(r["cotangent"], r["v_cot"], peer(0))
+    lat_move, cot_move = remote_of(r["v_lat_own"], r["v_lat"], peer(0)), remote_of(r["cotangent"], r["v_cot"], peer(0))
     kept_move = remote_of(r["v_kept_own"], r["v_kept"], sib)
-    lat_stay, cot_stay = here_of(r["latents"], r["v_lat"]), here_of(r["cotangent"], r["v_cot"])
+    cot_stay = here_of(r["cotangent"], r["v_cot"])
+    lat_copy = here(r["latents"], r["v_lat_own"])
+    asked_move = remote_of(r["v_asked_own"], r["v_asked"], peer(0))
     kept_stay = here_of(r["v_kept_own"], r["v_kept"])
     picture_stay = here_of(r["v_home"].at[s], picture.at[:, pl.ds(pl.multiple_of(base + s * LANES, LANES), LANES)])
 
-    @pl.when(c != t)
-    def _():
-        lat_move.start()
-
-    @pl.when(c == t)
-    def _():
-        lat_stay.start()
-        cot_stay.start()
-
-    pixels_copy = here(r["pixels"], r["v_pixels"])
-
-    mine, theirs = l, 1 - l
     own256 = 256 * c
     own_columns = pl.ds(pl.multiple_of(own256, LANES), 256)
     attend_far, out_w, up_far, down_far = r["w_attend_far"], r["w_out"], r["w_up_far"], r["w_down_far"]
@@ -222,31 +222,21 @@
         return pl.ds(pl.multiple_of(base_row + 16 * piece, 16), 16)
 
     shares = {
+        "attend": (lambda p: r["self_attend"].at[:, block(p, 64), own_columns], lambda p: attend_far.at[:, block(p, 64)]),
         "out": (lambda p: r["self_out"].at[rows16(own256, p)], lambda p: out_w.at[rows16(256, p)]),
         "up": (lambda p: r["self_up"].at[block(p, 64), own_columns], lambda p: up_far.at[block(p, 64), left]),
         "down": (lambda p: r["self_down"].at[rows16(own256, p)], lambda p: down_far.at[rows16(0, p)]),
     }
     first_piece = {name: remote(src(s), dst(s), over) for name, (src, dst) in shares.items()}
-
-    def attend_piece(k, p):
-        return attend_far.at[k, block(p, 512)]
-
-    across = {}
-    for k in range(3):
-        across["attend%d" % k] = remote(
-            r["self_attend"].at[k, block(theirs, 512), own_columns], attend_piece(k, theirs), over
-        )
-    onward = {}
-
-    def pass_on(*wanted):
-        for name in wanted:
-            across[name].wait_recv()
-            k = int(name[-1])
-            onward[name] = remote(attend_piece(k, mine), attend_piece(k, mine), beside)
-
-    def pass_rest(*wanted):
-        for name in wanted:
-            onward[name].wait_recv()
+    @pl.when(c == t)
+    def _():
+        cot_stay.start()
+
+    pixels_copy = here(r["pixels"], r["v_pixels"])
+    r["norm_gains"][...] = jnp.concatenate(
+        [row_of(r[name + "_gain"]) for name in ("query", "cross", "attend", "feed")] + [jnp.zeros((4, WIDE), F32)],
+        axis=0,
+    )
 
     pieces = {}
 
@@ -255,6 +245,10 @@
             first_piece[name].wait_recv()
             dst = shares[name][1]
             pieces[name] = [remote(dst(s), dst(s), plane(k)) for k in range(1, seq)]
+
+    def gathered(name):
+        for copy in pieces[name]:
+            copy.wait_recv()
 
     whole = {
         "out": (out_w.at[pl.ds(256, 256)], out_w.at[pl.ds(768, 256)]),
@@ -265,17 +259,12 @@
 
     def gather_pieces(*wanted):
         for name in wanted:
-            for copy in pieces[name]:
-                copy.wait_recv()
+            gathered(name)
             sib_quarter[name] = remote(*whole[name], sib)
 
     def arrived(*wanted):
         for name in wanted:
             sib_quarter[name].wait_recv()
-
-    @pl.when(c != t)
-    def _():
-        cot_move.start()
 
     pixels_copy.wait()
     pixels, normed = r["v_pixels"], r["v_normed"]
@@ -288,6 +277,7 @@
     def sum_step(i, total):
         return total + jnp.sum(pixels[features(i)].astype(F32), axis=0)
 
+    per_feature(r["pixel_gain"], r["v_gain"])
     zeros = jnp.zeros(pixels.shape[1:], F32)
     average = lax.fori_loop(0, channels // some, sum_step, zeros) * (1.0 / channels)
 
@@ -299,7 +289,7 @@
     inverse = lax.rsqrt(spread + EPS)
 
     def norm_step(i):
-        value = (pixels[features(i)].astype(F32) - average) * inverse * r["pixel_gain"][features(i)]
+        value = (pixels[features(i)].astype(F32) - average) * inverse * r["v_gain"][features(i), :][:, None, :]
         normed[pl.ds(pl.multiple_of(i * (some * 16), 16), some * 16), :] = value.reshape(some * 16, LANES)
 
     loop(channels // some, norm_step)
@@ -356,8 +346,6 @@
         here(r["self_out"].at[pl.ds(pl.multiple_of(256 - own256, LANES), 256)], out_w.at[pl.ds(512, 256)]).wait,
     ]
 
-    spread_pieces("out", "up", "down")
-
     def norm_rows(value_ref, gain, out_ref, also=None):
         def step(i):
             rows = block(i, 64)
@@ -370,38 +358,32 @@
     def each256(n, step):
         loop(n // 256, lambda i: step(block(i, 256)))
 
+    query_low, queries = r["v_query_low"], r["v_queries"]
+
+    def ask(lat_ref):
+        norm_rows(lat_ref, r["norm_gains"][0:1, :], query_low)
+
+        def query_step(columns):
+            queries[:, columns] = dot(query_low[...], r["w_query"][:, columns]).astype(B16)
+
+        each256(WIDE, query_step)
+
+    lat_copy.wait()
+    await_all("w_query")
+    ask(r["v_lat_own"])
+    r["v_asked_own"][...] = (dot_t(queries[...], r["w_key"][...]) * cross_scale).astype(B16)
+
     @pl.when(c != t)
     def _():
-        lat_move.wait_recv()
+        asked_move.start()
+        lat_move.start()
 
     @pl.when(c == t)
     def _():
-        lat_stay.wait()
-
-    store("latents_turned", r["v_lat"])
-    query_low, queries = r["v_query_low"], r["v_queries"]
-    norm_rows(r["v_lat"], r["norm_gains"][0:1, :], query_low)
-    await_all("w_query")
-
-    def query_step(columns):
-        queries[:, columns] = dot(query_low[...], r["w_query"][:, columns]).astype(B16)
-
-    each256(WIDE, query_step)
-    r["v_asked"][...] = (dot_t(queries[...], r["w_key"][...]) * cross_scale).astype(B16)
-    store("asked", r["v_asked"])
-    late = r["late_x"]
-    late_keep = [here_of(src, late.at[top]) for src in (query_low, queries)]
-    late_give = [remote_of(src, late.at[low], sib) for src in (queries, query_low)]
-
-    @pl.when(c == 0)
-    def _():
-        late_keep[0].start()
-        late_give[0].start()
-
-    @pl.when(c == 1)
-    def _():
-        late_keep[1].start()
-        late_give[1].start()
+        r["v_asked"][...] = r["v_asked_own"][...]
+        r["v_lat"][...] = r["v_lat_own"][...]
+
+    spread_pieces("attend")
 
     def chunk(k):
         return picture.at[:, pl.ds(pl.multiple_of(base + lax.rem(s - k + seq, seq) * LANES, LANES), LANES)]
@@ -424,6 +406,16 @@
         copy.wait_recv()
     store("picture", picture)
 
+    @pl.when(c != t)
+    def _():
+        cot_move.start()
+
+    spread_pieces("out", "up", "down")
+    @pl.when(c != t)
+    def _():
+        asked_move.wait_recv()
+
+    store("asked", r["v_asked"])
     scores, raised = r["v_scores"], r["v_raised"]
     r["v_top"][...] = jnp.full((ROWS, 1), -3.0e38, F32)
     r["v_total"][...] = jnp.zeros((ROWS, 1), F32)
@@ -467,6 +459,12 @@
     r["v_attended"][...] = dot(mixed.astype(B16), r["w_value"][...]).astype(B16)
     share("attended", r["v_attended"])
 
+    @pl.when(c != t)
+    def _():
+        lat_move.wait_recv()
+
+    store("latents_turned", r["v_lat"])
+
     def out_step(columns):
         r["v_after_cross"][:, columns] = r["v_lat"][:, columns].astype(F32) + dot(
             r["v_attended"][...], r["w_cross_out"][:, columns]
@@ -474,7 +472,6 @@
 
     each256(WIDE, out_step)
     store("after_cross", r["v_after_cross"])
-    pass_on("attend0")
     norm_rows(r["v_after_cross"], r["norm_gains"][1:2, :], r["v_cross_in"])
     share("cross_in", r["v_cross_in"])
     await_all("w_cross_up", "w_cross_down")
@@ -487,7 +484,6 @@
     each256(WIDE, up_step)
     store("cross_hidden", r["v_hidden"])
     share("cross_act", r["v_cross_act"])
-    pass_on("attend1")
 
     def down_step(columns):
         r["v_after_mlp"][:, columns] = r["v_after_cross"][:, columns] + dot(
@@ -500,8 +496,25 @@
     attend_in = r["v_attend_in"]
     norm_rows(r["v_after_mlp"], r["norm_gains"][2:3, :], attend_in)
     attend_copy = remote(attend_in.at[top], attend_in.at[low], sib)
+    @pl.when(c != t)
+    def _():
+        ask(r["v_lat"])
+
+    late = r["late_x"]
+    late_keep = [here_of(src, late.at[top]) for src in (query_low, queries)]
+    late_give = [remote_of(src, late.at[low], sib) for src in (queries, query_low)]
+
+    @pl.when(c == 0)
+    def _():
+        late_keep[0].start()
+        late_give[0].start()
+
+    @pl.when(c == 1)
+    def _():
+        late_keep[1].start()
+        late_give[1].start()
+
     await_all("attend_own")
-    pass_on("attend2")
     attend_copy.wait_recv()
     store("attend_in", attend_in)
     projected, probs = r["v_projected"], r["v_probs"]
@@ -521,7 +534,7 @@
 
     project(r["w_attend_own"], 0)
     loop(2, attend)
-    pass_rest("attend0", "attend1", "attend2")
+    gathered("attend")
     project(attend_far, 256)
     loop(2, lambda i: attend(i + 2))
     store("mixed", r["v_self"])
@@ -562,6 +575,7 @@
     @pl.when(c != t)
     def _():
         lat_move.wait_send()
+        asked_move.wait_send()
         cot_move.wait_send()
         away[0].wait_send()
 
@@ -600,7 +614,7 @@
         names.append(name)
         scratch.append(pltpu.VMEM(shape, dtype))
 
-    sems = (101, 38)
+    sems = (112, 38)
     names += list(FRONT_HBM) + list(FRONT_VMEM) + list(FRONT_OUT)
     for name in ("send", "recv", "local"):
         names.append(name)
@@ -616,12 +630,14 @@
     room("v_picture", (PAD, 4096))
     room("v_pixels", (261, 16, LANES))
     room("v_normed", (PAD * 16, LANES), F32)
+    room("v_gain", (384, LANES), F32)
     room("v_home", (16, PAD, LANES))
     room("v_kept", (8, 4096), F32)
     room("v_kept_own", (8, 4096), F32)
     room("v_scores", (ROWS, 4096), F32)
     room("v_raised", (8, ROWS, 512))
-    for name in ("lat", "cot", "query_low", "queries", "attended", "cross_in", "cross_act"):
+    room("v_asked_own", (ROWS, PAD))
+    for name in ("lat_own", "lat", "cot", "query_low", "queries", "attended", "cross_in", "cross_act"):
         room("v_" + name, (ROWS, WIDE))
     for name in ("after_cross", "hidden", "after_mlp", "after_attend"):
         room("v_" + name, (ROWS, WIDE), F32)
@@ -651,8 +667,18 @@
     return dict(zip(FRONT_OUT, result))
 
 
-LINKS = ("XA", "ZA", "L", "XB", "ZB", "O")
-SETS = {"S": ((0, 1, 2, 3, 4, 5), 32), "P": ((0, 3, 1, 4), 16), "Q": ((2, 5, 0, 3), 16)}
+X, Z, Y = ("XA", "XB"), ("ZA", "ZB"), ("L", "O")
+def rotated(k):
+    order = ("XA", "ZA", "L", "XB", "ZB", "O")
+    return tuple((bit,) for bit in order[k:] + order[:k])
+
+
+SETS = {
+    "S": (tuple(rotated(k) for k in range(6)), 32),
+    "P": (tuple(rotated(k) for k in (0, 3, 1, 4)), 16),
+    "Q": (tuple(rotated(k) for k in (2, 5, 0, 3)), 16),
+}
+BOTH = {X: "X2", Z: "Z2", Y: "T"}
 BACK_HBM = (
     ("cot", "cross_act", "cross_in", "attended", "late_x", "mixed_pixels", "mixed", "attend_in", "projected", "probs")
     + ("out_mine", "attend_far", "up_far", "down_far", "after_mlp", "after_attend", "cross_hidden", "after_cross")
@@ -687,6 +713,9 @@
         "ZB": (2 * l + c, (3 - z) * 4 + x, t),
         "L": (2 * (1 - l) + c, s, t),
         "O": (2 * (1 - l) + c, s, 1 - t),
+        "X2": (2 * l + c, z * 4 + lax.rem(x + 2, 4), t),
+        "Z2": (2 * l + c, lax.rem(z + 2, 4) * 4 + x, t),
+        "T": (2 * l + c, s, 1 - t),
         "C": (2 * l + 1 - c, s, t),
         "D": (2 * (1 - l) + 1 - c, s, t),
     }
@@ -697,8 +726,11 @@
     barrier = pltpu.get_barrier_semaphore()
     for device in partner.values():
         pl.semaphore_signal(barrier, inc=1, device_id=device, device_id_type=MESH)
+    def plane(k):
+        return (2 * l + c, lax.rem(s + k, seq), t)
+
     for k in range(1, seq):
-        pl.semaphore_signal(barrier, inc=1, device_id=peer(k), device_id_type=MESH)
+        pl.semaphore_signal(barrier, inc=1, device_id=plane(k), device_id_type=MESH)
 
     @pl.when(c != t)
     def _():
@@ -789,12 +821,13 @@
 
     class Part:
         def __init__(self, set_, q):
-            first, self.depth = SETS[set_][0][q], SETS[set_][1]
-            self.order = LINKS[first:] + LINKS[:first]
+            self.stages, self.depth = SETS[set_][0][q], SETS[set_][1]
             self.set, self.q, self.stage, self.n = set_, q, -1, 64
             self.key = "%s%d_" % (set_, q)
             self.cur = r[self.key + "buf"]
-            self.weight = {bit: 32 >> k for k, bit in enumerate(self.order)}
+            order = [bit for stage in self.stages for bit in stage]
+            self.weight = {bit: 32 >> k for k, bit in enumerate(order)}
+            self.done = False
 
         def index(self, **bits):
             return sum(value * self.weight[bit] for bit, value in bits.items())
@@ -802,9 +835,19 @@
         def begin(self):
             self.stage += 1
             k, n = self.stage, self.n
-            if k < 6:
+            if k < len(self.stages):
+                bits = self.stages[k]
                 self.into = r[self.key + "in%d" % k]
-                self.copies = [remote(self.cur.at[pl.ds(n // 2, n // 2)], self.into, partner[self.order[k]])]
+                if len(bits) == 1:
+                    ways = bits
+                else:
+                    ways = (bits[1], bits[0], BOTH[bits])
+                m = n // (len(ways) + 1)
+                self.n = m
+                self.copies = [
+                    remote(self.cur.at[pl.ds((j + 1) * m, m)], self.into.at[j], partner[way])
+                    for j, way in enumerate(ways)
+                ]
                 return
             count = len(SETS[self.set][0])
             dst = r["out_" + self.set].at[
@@ -817,16 +860,19 @@
         def finish(self):
             for copy in self.copies:
                 copy.wait_recv()
-            if self.stage == 6:
+            if self.stage == len(self.stages):
                 self.copy_here.wait()
+                self.done = True
                 return
-            self.n //= 2
-            cur, into = self.cur, self.into
+            cur, into, ways = self.cur, self.into, len(self.copies)
             m = min(self.n, 4)
 
             def step(i):
                 rows = pl.ds(i * m, m)
-                cur[rows] = (cur[rows].astype(F32) + into[rows].astype(F32)).astype(B16)
+                total = cur[rows].astype(F32)
+                for j in range(ways):
+                    total = total + into[j, rows].astype(F32)
+                cur[rows] = total.astype(B16)
 
             if self.n > m:
                 loop(self.n // m, step)
@@ -834,8 +880,10 @@
                 step(0)
 
         def advance(self):
+            if self.done:
+                return
             self.finish()
-            if self.stage < 6:
+            if not self.done:
                 self.begin()
 
     parts = {(set_, q): Part(set_, q) for set_ in SETS for q in range(len(SETS[set_][0]))}
@@ -1106,7 +1154,9 @@
         picture, raised = r["v_picture"][:, block(i, 512)], probs[i]
         change = (raised.astype(F32) * (dot(r["v_pull"][...], picture) - r["v_dot"][...])).astype(B16)
         r["v_sum"][...] += dot_t(change, picture)
-        to[:, block(at, 512)] = (dot(r["v_asked_t"][...], change) + dot(r["v_pull_t"][...], raised)).astype(B16)
+        grad = (dot(r["v_asked_t"][...], change) + dot(r["v_pull_t"][...], raised)).astype(B16)
+        for j in range(4):
+            to[4 * at + j] = grad[:, j * LANES : (j + 1) * LANES]
 
     loop(4, lambda i: pixel_chunk((1 - c) * 4 + i, r["grad_far"], i))
     grad_copy = remote(r["grad_far"], r["grad_in"], sib)
@@ -1123,31 +1173,51 @@
         r["v_asked"][...].astype(F32) * turned_sum + pull_f32 * r["v_mixed"][...], axis=0, keepdims=True
     )
 
+
     grad_copy.wait_recv()
 
     def grad_step(i):
-        rows = block(i, 16)
-        r["grad_own"][rows, :] = (r["grad_own"][rows, :].astype(F32) + r["grad_in"][rows, :].astype(F32)).astype(B16)
-
-    loop(PAD // 16, grad_step)
-
-    def homeward_of(k):
-        to = lax.rem(s + k, seq)
-        return remote_of(r["grad_own"].at[:, block(to, LANES)], r["home"].at[s], peer(k))
-
-    homeward = [homeward_of(k) for k in range(seq)]
-    stay = here_of(r["grad_own"].at[:, block(s, LANES)], r["home"].at[s])
+        r["grad_own"][i] = (r["grad_own"][i].astype(F32) + r["grad_in"][i].astype(F32)).astype(B16)
+
+    loop(seq, grad_step)
+
+    hops = [(i, j) for i in range(4) for j in range(4)]
+
+    def towards(i, j):
+        return 4 * lax.rem(z + i, 4) + lax.rem(x + j, 4)
+
+    def home_of(i, j, ref, sem):
+        to = towards(i, j)
+        return pltpu.make_async_remote_copy(
+            src_ref=ref.at[to],
+            dst_ref=r["home"].at[s],
+            send_sem=send.at[sem],
+            recv_sem=recv.at[sem],
+            device_id=(2 * l + c, to, t),
+            device_id_type=MESH,
+        )
+
+    first_sem = used[0]
+    used[0] += len(hops)
+    own_way = [home_of(i, j, r["grad_own"], first_sem + k) if k else None for k, (i, j) in enumerate(hops)]
+    far_way = [home_of(i, j, r["grad_relay"], first_sem + k) if k else None for k, (i, j) in enumerate(hops)]
+
+    def group(i):
+        return block(lax.rem(z + i, 4), 4)
+
+    crossing = [remote_of(r["grad_own"].at[group(i)], r["grad_relay"].at[group(i)], peer(0)) for i in range(4)]
+    stay, stay_far = here_of(r["grad_own"].at[s], r["home"].at[s]), here_of(r["grad_relay"].at[s], r["home"].at[s])
 
     @pl.when(c != t)
     def _():
-        homeward[0].start()
+        for copy in crossing:
+            copy.start()
 
     @pl.when(c == t)
     def _():
         stay.start()
-
-    for k in range(1, seq):
-        homeward[k].start()
+        for copy in own_way[1:]:
+            copy.start()
 
     await_all("x_attended", "y_out")
     product_rows(x4, r["y_out"], 512, "Q", 0)
@@ -1164,6 +1234,13 @@
     advance("S", 0, 1, 2)
     advance("P")
 
+    @pl.when(c != t)
+    def _():
+        for i in range(4):
+            crossing[i].wait_recv()
+            for j in range(4):
+                (far_way[4 * i + j] if i or j else stay_far).start()
+
     sent(*quarter_sends)
     latents, latgrad = r["v_feed_act"], r["v_feed_back"]
     load("latents_turned", latents)
@@ -1186,34 +1263,39 @@
         grad_stay.start()
 
     gain_buf, gain_in = r["gain_buf"], r["gain_in"]
+    gain_stages = [tuple(bits) + (BOTH[bits],) for bits in (X, Z, Y)] + [("C",)]
     gain_buf[0] = r["gains"][...]
-    gain_steps = LINKS + ("C",)
-    gain_copy = remote(gain_buf.at[0], gain_in.at[0], partner[gain_steps[0]])
+
+    def send_gains(k):
+        return [remote(gain_buf.at[k], gain_in.at[k, j], partner[way]) for j, way in enumerate(gain_stages[k])]
+
+    gain_copies = send_gains(0)
     live = [parts[key] for key in parts]
     k = 0
-    while live or k < 7:
-        if k < 7:
-            gain_copy.wait_recv()
-            total = gain_buf[k] + gain_in[k]
+    while live or k < 4:
+        if k < 4:
+            for copy in gain_copies:
+                copy.wait_recv()
+            total = gain_buf[k] + gain_in[k, 0]
+            if k < 3:
+                total = total + (gain_in[k, 1] + gain_in[k, 2])
             k += 1
-            if k < 7:
+            if k < 4:
                 gain_buf[k] = total
-                gain_copy = remote(gain_buf.at[k], gain_in.at[k], partner[gain_steps[k]])
+                gain_copies = send_gains(k)
             else:
                 r["out_gains"][...] = total
-        left_over = []
         for part in live:
-            last = part.stage == 6
             part.advance()
-            if not last:
-                left_over.append(part)
-        live = left_over
+        live = [part for part in live if not part.done]
 
     @pl.when(c != t)
     def _():
         out_move.wait()
         grad_move.wait()
-        homeward[0].wait()
+        stay_far.wait()
+        for copy in crossing:
+            copy.wait_send()
 
     @pl.when(c == t)
     def _():
@@ -1221,8 +1303,8 @@
         grad_stay.wait()
         stay.wait()
 
-    for k in range(1, seq):
-        homeward[k].wait()
+    for copy in own_way[1:]:
+        copy.wait()
     for copy in waits:
         copy.wait_send()
     assert not ready, tuple(ready)
@@ -1236,7 +1318,7 @@
         names.append(name)
         scratch.append(pltpu.VMEM(shape, dtype))
 
-    sems = (200, 96)
+    sems = (210, 58)
     names += list(BACK_HBM) + list(BACK_VMEM) + list(BACK_OUT)
     for name in ("send", "recv", "local"):
         names.append(name)
@@ -1270,17 +1352,18 @@
     room("v_asked_t", (PAD, ROWS))
     room("v_pull_t", (PAD, ROWS))
     room("v_dot", (ROWS, 1), F32)
-    for name in ("grad_own", "grad_far", "grad_in"):
-        room(name, (PAD, 16 * LANES))
+    for name in ("grad_own", "grad_far", "grad_in", "grad_relay"):
+        room(name, (16, PAD, LANES))
     room("gains", (8, WIDE), F32)
-    room("gain_buf", (7, 8, WIDE), F32)
-    room("gain_in", (7, 8, WIDE), F32)
-    for set_, (firsts, depth) in SETS.items():
-        for q in range(len(firsts)):
-            key = "%s%d_" % (set_, q)
-            room(key + "buf", (64, depth, 256))
-            for k in range(6):
-                room(key + "in%d" % k, (32 >> k, depth, 256))
+    room("gain_buf", (4, 8, WIDE), F32)
+    room("gain_in", (4, 3, 8, WIDE), F32)
+    for set_, (plans, depth) in SETS.items():
+        for q, stages in enumerate(plans):
+            key, n = "%s%d_" % (set_, q), 64
+            room(key + "buf", (n, depth, 256))
+            for k, bits in enumerate(stages):
+                n >>= len(bits)
+                room(key + "in%d" % k, (2 ** len(bits) - 1, n, depth, 256))
     anywhere = pl.BlockSpec(memory_space=pl.ANY)
     vmem = pl.BlockSpec(memory_space=pltpu.VMEM)
     result = pl.pallas_call(
@@ -1313,7 +1396,7 @@
     gain_rows, pixelgain, query_grad, key_grad, value_grad, crossout, crossup, crossdown = take(8)
     selfattend, selfout, selfup, selfdown = take(4)
     vmem = dict(zip(FINISH_IN, take(len(FINISH_IN))))
-    turned, high, grad, latgrad, sems = take(5)
+    turned, high, grad, latgrad, wide_gain, sems = take(6)
     pixels, home = vmem["pixels"], vmem["home"]
     channels = pixels.shape[0]
 
@@ -1332,6 +1415,7 @@
         return pl.ds(i * some, some)
 
     steps = channels // some
+    per_feature(gain, wide_gain)
     copies["pixels"].wait()
     zeros = jnp.zeros(pixels.shape[1:], F32)
     average = lax.fori_loop(
@@ -1350,7 +1434,7 @@
     def mean_step(i, totals):
         h = (pixels[features(i)].astype(F32) - average) * inverse
         rows = pl.ds(pl.multiple_of(i * (some * 16), 16), some * 16)
-        a = turned[rows, :].reshape(some, 16, LANES) * gain[features(i)]
+        a = turned[rows, :].reshape(some, 16, LANES) * wide_gain[features(i), :][:, None, :]
         high[features(i)] = h
         grad[features(i)] = a
         return totals[0] + jnp.sum(a, axis=0), totals[1] + jnp.sum(a * h, axis=0)
@@ -1401,7 +1485,7 @@
     rolled = pltpu.roll(gains[...], lax.rem(WIDE - 32 * mine, WIDE), 1)
     for k, ref in enumerate(gain_rows_of(gain_rows)):
         ref[...] = rolled[k : k + 1, :32]
-    pixelgain[...] = gains[4:5, :channels]
+    pixelgain[...] = gains[4:5, :channels] / row_of(gain)
     straight.wait()
     pixels_out.wait()
     latents_out.wait()
@@ -1446,6 +1530,7 @@
             pltpu.VMEM(pixels.shape, F32),
             pltpu.VMEM(pixels.shape, F32),
             pltpu.VMEM((ROWS, WIDE), F32),
+            pltpu.VMEM((384, LANES), F32),
             pltpu.SemaphoreType.DMA((len(FINISH_IN) + 3,)),
         ],
         compiler_params=pltpu.CompilerParams(vmem_limit_bytes=60 * MIB),
@@ -1490,8 +1575,11 @@
         "self_out": self_out,
         "self_up": self_up,
         "self_down": self_down,
-        "norm_gains": jnp.stack([query_gain, cross_gain, attend_gain, feed_gain]).astype(F32),
-        "pixel_gain": jnp.broadcast_to(pixel_gain.astype(F32)[:, None, None], (channels, 1, LANES)),
+        "query_gain": query_gain,
+        "cross_gain": cross_gain,
+        "attend_gain": attend_gain,
+        "feed_gain": feed_gain,
+        "pixel_gain": pixel_gain,
         "key_mask": key_mask,
         "crop_bounds": crop_bounds,
     }
@@ -1519,7 +1607,7 @@
         latents_grad[None],
         jnp.transpose(pixels_grad, (1, 2, 0)),
         gain_rows[0],
-        pixelgain[0] / pixel_gain.astype(F32),
+        pixelgain[0],
         gain_rows[1],
         gain_rows[2],
         gain_rows[3],

time: 208 us -> 193 us (0.928)
  Pallas kernels: 199 us -> 190 us
  local copies, waits for them, and re-layouts: 5.77 us -> 1.35 us
    pallas_call x1, Pallas kernels: 80 us -> 75.2 us  [front(): pl.pallas_call(functools.partial(front_kernel, tuple(names), sems), out_s...]
    pallas_call x1, Pallas kernels: 110 us -> 106 us  [back_and_reduce(): pl.pallas_call(functools.partial(back_kernel, tuple(names), sems), out_sh...]
    another operation x4 -> x0, local copies, waits for them, and re-layouts: 2.74 us -> none  [shards(): jnp.stack([query_gain, cross_gain, attend_gain, feed_gain]).astype(F32)]
where the time goes in v2:
time: 193 us
  Pallas kernels  190 us (98%)
    pallas_call x1, Pallas kernels, back_and_reduce(): pl.pallas_call(functools.partial(back_kernel, tuple(names), sems), out_sh...  106 us
    pallas_call x1, Pallas kernels, front(): pl.pallas_call(functools.partial(front_kernel, tuple(names), sems), out_s...  75.2 us
    pallas_call x1, Pallas kernels, finish(): pl.pallas_call(finish_kernel, out_shape=[jax.ShapeDtypeStruct(pixels.shap...  8.23 us

profile of v2, /device:TPU:1, one launch (start us, length us, event | category | flops | bytes accessed | tf_op | source)
XLA Modules:
  0.0 193.0 jit_solution(12230660967092443773)
XLA Ops:
  0.7 75.2 %front.1 = (bf16[512,1024]{1,0:T(8,128)(2,1)}, bf16[512,1024]{1,0:T(8,128)(2,1)}, bf16[512,1024]{1,0:T(8,128)(2,1)}, bf16[512,1024]{1,0:T(8,128)(2,1)}, bf16[512...) custom-call(bf16[261,16,128]{2,1,0:T(8,128)(2,1)} %bitcast.18, ...), custom_call_target="tpu_custom_call" | custom-call | tf_op jit(solution)/shard_map/front/pallas_call | solution.py:658
  75.9 106.2 %back_and_reduce.1 = (bf16[64,3072]{1,0:T(8,128)(2,1)}, bf16[32,2048]{1,0:T(8,128)(2,1)}, bf16[32,2048]{1,0:T(8,128)(2,1)}, bf16[16,272,128]{2,1,0:T(8,128)(2,1)...) custom-call(bf16[512,1024]{1,0:T(8,128)(2,1)} %get-tuple-element.68.refs_0_, ...), custom_call_target="tpu_custom_call" | custom-call | tf_op jit(solution)/shard_map/back_and_reduce/pallas_call | solution.py:1369
  182.1 8.2 %finish.1 = (f32[261,16,128]{2,1,0:T(8,128)}, f32[256,1024]{1,0:T(8,128)}, bf16[256,1024]{1,0:T(8,128)(2,1)}, f32[4,32]{1,0:T(4,128)}, f32[1,261]{1,0:T(1,128)},...) custom-call(bf16[261,16,128]{2,1,0:T(8,128)(2,1)} %bitcast.19, ...), custom_call_target="tpu_custom_call" | custom-call | tf_op jit(solution)/shard_map/finish/pallas_call | solution.py:1517
  190.4 1.3 reduce
  191.6 1.3 slice_bitcast_fusion

commit v3 on v2

--- a/solution.py
+++ b/solution.py
@@ -1393,7 +1393,8 @@
     hbm = dict(zip(FINISH_IN, take(len(FINISH_IN))))
     gain, gains = take(2)
     results = dict(zip(FINISH_OUT, take(len(FINISH_OUT))))
-    gain_rows, pixelgain, query_grad, key_grad, value_grad, crossout, crossup, crossdown = take(8)
+    gain_rows = take(4)
+    pixelgain, query_grad, key_grad, value_grad, crossout, crossup, crossdown = take(7)
     selfattend, selfout, selfup, selfdown = take(4)
     vmem = dict(zip(FINISH_IN, take(len(FINISH_IN))))
     turned, high, grad, latgrad, wide_gain, sems = take(6)
@@ -1409,7 +1410,7 @@
     for copy in copies.values():
         copy.start()
 
-    some = 9
+    some = 29
 
     def features(i):
         return pl.ds(i * some, some)
@@ -1483,24 +1484,19 @@
 
     mine = 2 * lax.axis_index("seq") + lax.axis_index("tensor")
     rolled = pltpu.roll(gains[...], lax.rem(WIDE - 32 * mine, WIDE), 1)
-    for k, ref in enumerate(gain_rows_of(gain_rows)):
-        ref[...] = rolled[k : k + 1, :32]
-    pixelgain[...] = gains[4:5, :channels] / row_of(gain)
+    for k, ref in enumerate(gain_rows):
+        ref[...] = rolled[k : k + 1, :32].reshape(32)
+    pixelgain[...] = (gains[4:5, :channels] / row_of(gain)).reshape(channels)
     straight.wait()
     pixels_out.wait()
     latents_out.wait()
 
 
-def gain_rows_of(ref):
-    return [ref.at[pl.ds(k, 1)] for k in range(4)]
-
-
 def finish(given):
     pixels = given["pixels"]
     channels, images, rows = pixels.shape
-    small = [
-        (4, 32),
-        (1, channels),
+    small = [(32,)] * 4 + [
+        (channels,),
         (32, WIDE),
         (32, channels),
         (32, channels),
@@ -1589,7 +1585,10 @@
         pixels_grad,
         latents_grad,
         latents_out,
-        gain_rows,
+        querygain,
+        crossgain,
+        attendgain,
+        feedgain,
         pixelgain,
         queryweight_grad,
         keyweight_grad,
@@ -1606,11 +1605,11 @@
         latents_out[None],
         latents_grad[None],
         jnp.transpose(pixels_grad, (1, 2, 0)),
-        gain_rows[0],
-        pixelgain[0],
-        gain_rows[1],
-        gain_rows[2],
-        gain_rows[3],
+        querygain,
+        pixelgain,
+        crossgain,
+        attendgain,
+        feedgain,
         queryweight_grad,
         keyweight_grad.T,
         valueweight_grad.T,

time: 193 us -> 191 us (0.990)
  no operation moved by 1% of the time
where the time goes in v3:
time: 191 us; the launch traced here: 190 us
  Pallas kernels  189 us (99%)
    pallas_call x1, Pallas kernels, back_and_reduce(): pl.pallas_call(functools.partial(back_kernel, tuple(names), sems), out_sh...  106 us
    pallas_call x1, Pallas kernels, front(): pl.pallas_call(functools.partial(front_kernel, tuple(names), sems), out_s...  75.2 us
    pallas_call x1, Pallas kernels, finish(): pl.pallas_call(finish_kernel, out_shape=[jax.ShapeDtypeStruct(pixels.shap...  7.86 us

profile of v3, /device:TPU:1, one launch (start us, length us, event | category | flops | bytes accessed | tf_op | source)
XLA Modules:
  0.0 190.3 jit_solution(10115392571783444445)
XLA Ops:
  0.7 75.2 %front.1 = (bf16[512,1024]{1,0:T(8,128)(2,1)}, bf16[512,1024]{1,0:T(8,128)(2,1)}, bf16[512,1024]{1,0:T(8,128)(2,1)}, bf16[512,1024]{1,0:T(8,128)(2,1)}, bf16[512...) custom-call(bf16[261,16,128]{2,1,0:T(8,128)(2,1)} %bitcast.10, ...), custom_call_target="tpu_custom_call" | custom-call | tf_op jit(solution)/shard_map/front/pallas_call | solution.py:658
  75.9 106.3 %back_and_reduce.1 = (bf16[64,3072]{1,0:T(8,128)(2,1)}, bf16[32,2048]{1,0:T(8,128)(2,1)}, bf16[32,2048]{1,0:T(8,128)(2,1)}, bf16[16,272,128]{2,1,0:T(8,128)(2,1)...) custom-call(bf16[512,1024]{1,0:T(8,128)(2,1)} %get-tuple-element.71.refs_0_, ...), custom_call_target="tpu_custom_call" | custom-call | tf_op jit(solution)/shard_map/back_and_reduce/pallas_call | solution.py:1369
  182.2 7.9 %finish.1 = (f32[261,16,128]{2,1,0:T(8,128)}, f32[256,1024]{1,0:T(8,128)}, bf16[256,1024]{1,0:T(8,128)(2,1)}, f32[32]{0:T(128)}, f32[32]{0:T(128)}, /*index=5*/f...) custom-call(bf16[261,16,128]{2,1,0:T(8,128)(2,1)} %bitcast.11, ...), custom_call_target="tpu_custom_call" | custom-call | tf_op jit(solution)/shard_map/finish/pallas_call | solution.py:1513

commit v4 on v3

--- a/solution.py
+++ b/solution.py
@@ -138,17 +138,16 @@
         return (2 * l + c, lax.rem(s + k, seq), t)
 
     for k in range(1, seq):
-        pl.semaphore_signal(barrier, inc=1, device_id=peer(k), device_id_type=MESH)
         pl.semaphore_signal(barrier, inc=1, device_id=plane(k), device_id_type=MESH)
 
     @pl.when(c != t)
     def _():
         pl.semaphore_signal(barrier, inc=1, device_id=peer(0), device_id_type=MESH)
-        pl.semaphore_wait(barrier, 1 + 2 * seq)
+        pl.semaphore_wait(barrier, 2 + seq)
 
     @pl.when(c == t)
     def _():
-        pl.semaphore_wait(barrier, 2 * seq)
+        pl.semaphore_wait(barrier, 1 + seq)
 
     used = [0, 0]
     waits, stores = [], []
@@ -194,25 +193,45 @@
                 wait()
 
     base = pl.multiple_of(c * (seq * LANES), LANES)
-    far = pl.multiple_of(t * (seq * LANES), LANES)
     picture = r["v_picture"]
 
-    def away_of(k):
-        return remote_of(
-            r["v_home"].at[lax.rem(s + k, seq)],
-            picture.at[:, pl.ds(pl.multiple_of(far + s * LANES, LANES), LANES)],
-            peer(k),
+    z, x = lax.div(s, 4), lax.rem(s, 4)
+    hops = [(i, j) for i in range(4) for j in range(4)]
+
+    def towards(i, j, sign=1):
+        return 4 * lax.rem(z + sign * i + 4, 4) + lax.rem(x + sign * j + 4, 4)
+
+    def columns_of(source):
+        return picture.at[:, pl.ds(pl.multiple_of(base + source * LANES, LANES), LANES)]
+
+    own_way = [remote_of(r["v_home"].at[towards(i, j)], columns_of(s), (2 * l + c, towards(i, j), t)) for i, j in hops]
+    first_sem = used[0] - len(hops)
+    far_way = [
+        pltpu.make_async_remote_copy(
+            src_ref=r["v_relay"].at[towards(i, j)],
+            dst_ref=columns_of(s),
+            send_sem=send.at[first_sem + k],
+            recv_sem=recv.at[first_sem + k],
+            device_id=(2 * l + c, towards(i, j), t),
+            device_id_type=MESH,
         )
-
-    away = [away_of(k) for k in range(seq)]
+        for k, (i, j) in enumerate(hops)
+    ]
+
+    def group(i):
+        return block(lax.rem(z + i, 4), 4)
+
+    crossing = [remote_of(r["v_home"].at[group(i)], r["v_relay"].at[group(i)], peer(0)) for i in range(4)]
     lat_move, cot_move = remote_of(r["v_lat_own"], r["v_lat"], peer(0)), remote_of(r["cotangent"], r["v_cot"], peer(0))
     kept_move = remote_of(r["v_kept_own"], r["v_kept"], sib)
     cot_stay = here_of(r["cotangent"], r["v_cot"])
     lat_copy = here(r["latents"], r["v_lat_own"])
     asked_move = remote_of(r["v_asked_own"], r["v_asked"], peer(0))
     kept_stay = here_of(r["v_kept_own"], r["v_kept"])
-    picture_stay = here_of(r["v_home"].at[s], picture.at[:, pl.ds(pl.multiple_of(base + s * LANES, LANES), LANES)])
-
+    picture_stay = here_of(r["v_home"].at[s], columns_of(s))
+    picture_cross = here_of(r["v_relay"].at[s], columns_of(s))
+
+    z, x = lax.div(s, 4), lax.rem(s, 4)
     own256 = 256 * c
     own_columns = pl.ds(pl.multiple_of(own256, LANES), 256)
     attend_far, out_w, up_far, down_far = r["w_attend_far"], r["w_out"], r["w_up_far"], r["w_down_far"]
@@ -222,12 +241,18 @@
         return pl.ds(pl.multiple_of(base_row + 16 * piece, 16), 16)
 
     shares = {
-        "attend": (lambda p: r["self_attend"].at[:, block(p, 64), own_columns], lambda p: attend_far.at[:, block(p, 64)]),
-        "out": (lambda p: r["self_out"].at[rows16(own256, p)], lambda p: out_w.at[rows16(256, p)]),
-        "up": (lambda p: r["self_up"].at[block(p, 64), own_columns], lambda p: up_far.at[block(p, 64), left]),
-        "down": (lambda p: r["self_down"].at[rows16(own256, p)], lambda p: down_far.at[rows16(0, p)]),
+        "attend": (lambda p: r["self_attend"].at[:, block(p, 64), own_columns], lambda p, n=1: attend_far.at[:, block(p, 64 * n)]),
+        "out": (lambda p: r["self_out"].at[rows16(own256, p)], lambda p, n=1: out_w.at[pl.ds(pl.multiple_of(256 + 16 * n * p, 16), 16 * n)]),
+        "up": (lambda p: r["self_up"].at[block(p, 64), own_columns], lambda p, n=1: up_far.at[block(p, 64 * n), left]),
+        "down": (lambda p: r["self_down"].at[rows16(own256, p)], lambda p, n=1: down_far.at[block(p, 16 * n)]),
     }
-    first_piece = {name: remote(src(s), dst(s), over) for name, (src, dst) in shares.items()}
+
+    def along(axis, k):
+        at = z * 4 + lax.rem(x + k, 4) if axis == "x" else lax.rem(z + k, 4) * 4 + x
+        return (2 * l + c, at, t)
+
+    plans = {name: ("z", 4 * x + z, "x", x) if name == "attend" else ("x", 4 * z + x, "z", z) for name in shares}
+    first_piece = {name: remote(src(plans[name][1]), dst(plans[name][1]), over) for name, (src, dst) in shares.items()}
     @pl.when(c == t)
     def _():
         cot_stay.start()
@@ -238,16 +263,25 @@
         axis=0,
     )
 
-    pieces = {}
+    pieces, fours = {}, {}
 
     def spread_pieces(*wanted):
         for name in wanted:
             first_piece[name].wait_recv()
-            dst = shares[name][1]
-            pieces[name] = [remote(dst(s), dst(s), plane(k)) for k in range(1, seq)]
+            axis, p, _, _ = plans[name]
+            at = shares[name][1](p)
+            pieces[name] = [remote(at, at, along(axis, k)) for k in range(1, 4)]
+
+    def spread_fours(*wanted):
+        for name in wanted:
+            for copy in pieces[name]:
+                copy.wait_recv()
+            _, _, axis, p = plans[name]
+            at = shares[name][1](p, 4)
+            fours[name] = [remote(at, at, along(axis, k)) for k in range(1, 4)]
 
     def gathered(name):
-        for copy in pieces[name]:
+        for copy in fours[name]:
             copy.wait_recv()
 
     whole = {
@@ -295,23 +329,18 @@
     loop(channels // some, norm_step)
     normed[channels * 16 :, :] = jnp.zeros(((PAD - channels) * 16, LANES), F32)
 
-    def turn_image(k):
-        image = lax.rem(s + k, seq)
-        r["v_home"][image] = normed[pl.ds(image, PAD, stride=16), :].astype(B16)
-
-    turn_image(0)
-
-    @pl.when(c != t)
-    def _():
-        away[0].start()
-
-    @pl.when(c == t)
-    def _():
-        picture_stay.start()
-
-    for k in range(1, seq):
-        turn_image(k)
-        away[k].start()
+    for i in range(4):
+        for j in range(4):
+            image = towards(i, j)
+            r["v_home"][image] = normed[pl.ds(image, PAD, stride=16), :].astype(B16)
+
+            @pl.when(c == t)
+            def _():
+                (own_way[4 * i + j] if i or j else picture_stay).start()
+
+        @pl.when(c != t)
+        def _():
+            crossing[i].start()
 
     start, count = r["crop_bounds"][:, 0:1], r["crop_bounds"][:, 1:2]
     lanes = lax.broadcasted_iota(jnp.int32, (1, LANES), 1)
@@ -383,34 +412,36 @@
         r["v_asked"][...] = r["v_asked_own"][...]
         r["v_lat"][...] = r["v_lat_own"][...]
 
-    spread_pieces("attend")
-
-    def chunk(k):
-        return picture.at[:, pl.ds(pl.multiple_of(base + lax.rem(s - k + seq, seq) * LANES, LANES), LANES)]
-
     @pl.when(c != t)
     def _():
-        away[0].wait_recv()
+        for i in range(4):
+            crossing[i].wait_recv()
+            for j in range(4):
+                (far_way[4 * i + j] if i or j else picture_cross).start()
         kept_move.wait_recv()
+        picture_cross.wait()
 
     @pl.when(c == t)
     def _():
+        kept_stay.wait()
         picture_stay.wait()
-        kept_stay.wait()
-
-    passed = [remote(chunk(0), chunk(0), sib)]
-    for k in range(1, seq):
-        away[k].wait_recv()
-        passed.append(remote(chunk(k), chunk(k), sib))
+
+    spread_pieces("attend", "out", "up", "down")
+    passed = []
+    for k, (i, j) in enumerate(hops):
+        if k > 0:
+            own_way[k].wait_recv()
+        arrived_at = columns_of(towards(i, j, -1))
+        passed.append(remote(arrived_at, arrived_at, sib))
     for copy in passed:
         copy.wait_recv()
+    spread_fours("attend")
     store("picture", picture)
 
     @pl.when(c != t)
     def _():
         cot_move.start()
 
-    spread_pieces("out", "up", "down")
     @pl.when(c != t)
     def _():
         asked_move.wait_recv()
@@ -457,6 +488,7 @@
     share("mixed_pixels", r["v_mixed_pixels"], r["v_mixed_pixels_give"])
     await_all("w_cross_out")
     r["v_attended"][...] = dot(mixed.astype(B16), r["w_value"][...]).astype(B16)
+    spread_fours("out", "up", "down")
     share("attended", r["v_attended"])
 
     @pl.when(c != t)
@@ -577,7 +609,8 @@
         lat_move.wait_send()
         asked_move.wait_send()
         cot_move.wait_send()
-        away[0].wait_send()
+        for copy in crossing:
+            copy.wait_send()
 
     @pl.when(c == t)
     def _():
@@ -595,8 +628,8 @@
         late_give[1].wait_send()
         late_give[0].wait_recv()
 
-    for k in range(1, seq):
-        away[k].wait_send()
+    for copy in own_way[1:]:
+        copy.wait_send()
     for copy in shared:
         copy.wait_recv()
     for copy in waits:
@@ -614,7 +647,7 @@
         names.append(name)
         scratch.append(pltpu.VMEM(shape, dtype))
 
-    sems = (112, 38)
+    sems = (80, 39)
     names += list(FRONT_HBM) + list(FRONT_VMEM) + list(FRONT_OUT)
     for name in ("send", "recv", "local"):
         names.append(name)
@@ -632,6 +665,7 @@
     room("v_normed", (PAD * 16, LANES), F32)
     room("v_gain", (384, LANES), F32)
     room("v_home", (16, PAD, LANES))
+    room("v_relay", (16, PAD, LANES))
     room("v_kept", (8, 4096), F32)
     room("v_kept_own", (8, 4096), F32)
     room("v_scores", (ROWS, 4096), F32)

time: 191 us -> 187 us (0.979)
  Pallas kernels: 189 us -> 186 us
    pallas_call x1, Pallas kernels: 75.2 us -> 67.7 us  [front(): pl.pallas_call(functools.partial(front_kernel, tuple(names), sems), out_s...]
    pallas_call x1, Pallas kernels: 106 us -> 110 us  [back_and_reduce(): pl.pallas_call(functools.partial(back_kernel, tuple(names), sems), out_sh...]
where the time goes in v4:
time: 187 us
  Pallas kernels  186 us (99%)
    pallas_call x1, Pallas kernels, back_and_reduce(): pl.pallas_call(functools.partial(back_kernel, tuple(names), sems), out_sh...  110 us
    pallas_call x1, Pallas kernels, front(): pl.pallas_call(functools.partial(front_kernel, tuple(names), sems), out_s...  67.7 us
    pallas_call x1, Pallas kernels, finish(): pl.pallas_call(finish_kernel, out_shape=[jax.ShapeDtypeStruct(pixels.shap...  7.86 us

profile of v4, /device:TPU:1, one launch (start us, length us, event | category | flops | bytes accessed | tf_op | source)
XLA Modules:
  0.0 186.7 jit_solution(15835596843292953203)
XLA Ops:
  0.7 67.7 %front.1 = (bf16[512,1024]{1,0:T(8,128)(2,1)}, bf16[512,1024]{1,0:T(8,128)(2,1)}, bf16[512,1024]{1,0:T(8,128)(2,1)}, bf16[512,1024]{1,0:T(8,128)(2,1)}, bf16[512...) custom-call(bf16[261,16,128]{2,1,0:T(8,128)(2,1)} %bitcast.10, ...), custom_call_target="tpu_custom_call" | custom-call | tf_op jit(solution)/shard_map/front/pallas_call | solution.py:692
  68.3 110.3 %back_and_reduce.1 = (bf16[64,3072]{1,0:T(8,128)(2,1)}, bf16[32,2048]{1,0:T(8,128)(2,1)}, bf16[32,2048]{1,0:T(8,128)(2,1)}, bf16[16,272,128]{2,1,0:T(8,128)(2,1)...) custom-call(bf16[512,1024]{1,0:T(8,128)(2,1)} %get-tuple-element.71.refs_0_, ...), custom_call_target="tpu_custom_call" | custom-call | tf_op jit(solution)/shard_map/back_and_reduce/pallas_call | solution.py:1403
  178.6 7.9 %finish.1 = (f32[261,16,128]{2,1,0:T(8,128)}, f32[256,1024]{1,0:T(8,128)}, bf16[256,1024]{1,0:T(8,128)(2,1)}, f32[32]{0:T(128)}, f32[32]{0:T(128)}, /*index=5*/f...) custom-call(bf16[261,16,128]{2,1,0:T(8,128)(2,1)} %bitcast.11, ...), custom_call_target="tpu_custom_call" | custom-call | tf_op jit(solution)/shard_map/finish/pallas_call | solution.py:1547

commit v5 on v4

--- a/solution.py
+++ b/solution.py
@@ -721,9 +721,9 @@
 )
 BACK_VMEM = ("inverse_total", "any_kept", "norm_gains")
 BACK_OUT = {
-    "out_S": ((64, 2 * 6 * 256), B16),
-    "out_P": ((32, 2 * 4 * 256), B16),
-    "out_Q": ((32, 2 * 4 * 256), B16),
+    "out_S": ((6, 64, 512), B16),
+    "out_P": ((4, 32, 512), B16),
+    "out_Q": ((4, 32, 512), B16),
     "home": ((16, PAD, LANES), B16),
     "latents_home": ((ROWS, WIDE), B16),
     "latgrad_home": ((ROWS, WIDE), B16),
@@ -853,6 +853,8 @@
     load("asked", r["v_asked"])
     load("mixed_pixels", r["y_mixed_pixels"])
 
+    missing, ends = {set_: len(SETS[set_][0]) for set_ in SETS}, []
+
     class Part:
         def __init__(self, set_, q):
             self.stages, self.depth = SETS[set_][0][q], SETS[set_][1]
@@ -883,21 +885,22 @@
                     for j, way in enumerate(ways)
                 ]
                 return
-            count = len(SETS[self.set][0])
-            dst = r["out_" + self.set].at[
-                pl.ds(pl.multiple_of(l * self.depth, self.depth), self.depth),
-                pl.ds(pl.multiple_of((count * c + self.q) * 256, LANES), 256),
-            ]
-            self.copies = [remote(self.cur.at[0], dst, partner[way]) for way in ("L", "C", "D")]
-            self.copy_here = here(self.cur.at[0], dst)
+            r["fin_" + self.set][self.q] = self.cur[0]
+            self.done = True
+            missing[self.set] -= 1
+            if not missing[self.set]:
+                src = r["fin_" + self.set]
+                dst = r["out_" + self.set].at[
+                    :,
+                    pl.ds(pl.multiple_of(l * self.depth, self.depth), self.depth),
+                    pl.ds(pl.multiple_of(c * 256, LANES), 256),
+                ]
+                ends.extend(remote(src, dst, partner[way]).wait_recv for way in ("L", "C", "D"))
+                ends.append(here(src, dst).wait)
 
         def finish(self):
             for copy in self.copies:
                 copy.wait_recv()
-            if self.stage == len(self.stages):
-                self.copy_here.wait()
-                self.done = True
-                return
             cur, into, ways = self.cur, self.into, len(self.copies)
             m = min(self.n, 4)
 
@@ -1322,6 +1325,8 @@
         for part in live:
             part.advance()
         live = [part for part in live if not part.done]
+    for wait in ends:
+        wait()
 
     @pl.when(c != t)
     def _():
@@ -1352,7 +1357,7 @@
         names.append(name)
         scratch.append(pltpu.VMEM(shape, dtype))
 
-    sems = (210, 58)
+    sems = (177, 47)
     names += list(BACK_HBM) + list(BACK_VMEM) + list(BACK_OUT)
     for name in ("send", "recv", "local"):
         names.append(name)
@@ -1392,6 +1397,7 @@
     room("gain_buf", (4, 8, WIDE), F32)
     room("gain_in", (4, 3, 8, WIDE), F32)
     for set_, (plans, depth) in SETS.items():
+        room("fin_" + set_, (len(plans), depth, 256))
         for q, stages in enumerate(plans):
             key, n = "%s%d_" % (set_, q), 64
             room(key + "buf", (n, depth, 256))
@@ -1493,28 +1499,23 @@
     for name in ("out_S", "out_P", "out_Q", "key_wide"):
         copies[name].wait()
     out_s, out_p, out_q = vmem["out_S"], vmem["out_P"], vmem["out_Q"]
-    late = [out_q[:, 512:1024], out_q[:, 1536:2048]]
-    query_grad[...] = dot(late[0][:, :PAD], vmem["key_wide"][...])
-    key_grad[...] = late[1][:, :channels].astype(F32)
-    value_grad[:, :LANES] = late[0][:, 384:].astype(F32)
-    value_grad[:, LANES : 2 * LANES] = late[1][:, 384:].astype(F32)
-    value_grad[:, 2 * LANES :] = late[0][:, 256:384].astype(F32)[:, 16 : 16 + channels - 2 * LANES]
-    for k, ref in enumerate((crossdown, crossup)):
+    late = [[out_q[2 + k, :, pl.ds(256 * core, 256)] for k in range(2)] for core in range(2)]
+    key_wide = vmem["key_wide"]
+    query_grad[...] = dot(late[0][0], key_wide[:256, :]) + dot(late[0][1][:, :16], key_wide[256:, :])
+    key_grad[:, : 2 * LANES] = late[1][0].astype(F32)
+    key_grad[:, 2 * LANES :] = late[1][1].astype(F32)[:, : channels - 2 * LANES]
+    value_grad[:, :LANES] = late[0][1][:, LANES:].astype(F32)
+    value_grad[:, LANES : 2 * LANES] = late[1][1][:, LANES:].astype(F32)
+    value_grad[:, 2 * LANES :] = late[0][1].astype(F32)[:, 16 : 16 + channels - 2 * LANES]
+    for ref, out, first in ((crossdown, out_p, 0), (crossup, out_p, 2), (crossout, out_q, 0)):
         for core in range(2):
-            ref[:, pl.ds(512 * core, 512)] = out_p[:, pl.ds(1024 * core + 512 * k, 512)].astype(F32)
-    for core in range(2):
-        crossout[:, pl.ds(512 * core, 512)] = out_q[:, pl.ds(1024 * core, 512)].astype(F32)
-
-    def item(k, core):
-        return out_s[:, pl.ds(1536 * core + 256 * k, 256)].astype(F32)
-
-    for core in range(2):
-        columns = pl.ds(256 * core, 256)
-        selfdown[:, columns] = item(0, core)
-        selfup[:, columns] = item(1, core)
-        selfout[:, columns] = item(2, core)
-        for k in range(3):
-            selfattend[k, :, columns] = item(3 + k, core)
+            for k in range(2):
+                ref[:, pl.ds(512 * core + 256 * k, 256)] = out[first + k, :, pl.ds(256 * core, 256)].astype(F32)
+    selfdown[...] = out_s[0].astype(F32)
+    selfup[...] = out_s[1].astype(F32)
+    selfout[...] = out_s[2].astype(F32)
+    for k in range(3):
+        selfattend[k] = out_s[3 + k].astype(F32)
 
     mine = 2 * lax.axis_index("seq") + lax.axis_index("tensor")
     rolled = pltpu.roll(gains[...], lax.rem(WIDE - 32 * mine, WIDE), 1)

time: 187 us -> 188 us (level)
  no operation moved by 1% of the time
where the time goes in v5:
time: 188 us; the launch traced here: 187 us
  Pallas kernels  186 us (99%)
    pallas_call x1, Pallas kernels, back_and_reduce(): pl.pallas_call(functools.partial(back_kernel, tuple(names), sems), out_sh...  111 us
    pallas_call x1, Pallas kernels, front(): pl.pallas_call(functools.partial(front_kernel, tuple(names), sems), out_s...  67.7 us
    pallas_call x1, Pallas kernels, finish(): pl.pallas_call(finish_kernel, out_shape=[jax.ShapeDtypeStruct(pixels.shap...  7.86 us

profile of v5, /device:TPU:1, one launch (start us, length us, event | category | flops | bytes accessed | tf_op | source)
XLA Modules:
  0.0 187.2 jit_solution(18282992502670953141)
XLA Ops:
  0.7 67.7 %front.1 = (bf16[512,1024]{1,0:T(8,128)(2,1)}, bf16[512,1024]{1,0:T(8,128)(2,1)}, bf16[512,1024]{1,0:T(8,128)(2,1)}, bf16[512,1024]{1,0:T(8,128)(2,1)}, bf16[512...) custom-call(bf16[261,16,128]{2,1,0:T(8,128)(2,1)} %bitcast.10, ...), custom_call_target="tpu_custom_call" | custom-call | tf_op jit(solution)/shard_map/front/pallas_call | solution.py:692
  68.3 110.8 %back_and_reduce.1 = (bf16[6,64,512]{2,1,0:T(8,128)(2,1)}, bf16[4,32,512]{2,1,0:T(8,128)(2,1)}, bf16[4,32,512]{2,1,0:T(8,128)(2,1)}, bf16[16,272,128]{2,1,0:T(8,...) custom-call(bf16[512,1024]{1,0:T(8,128)(2,1)} %get-tuple-element.71.refs_0_, ...), custom_call_target="tpu_custom_call" | custom-call | tf_op jit(solution)/shard_map/back_and_reduce/pallas_call | solution.py:1409
  179.2 7.9 %finish.1 = (f32[261,16,128]{2,1,0:T(8,128)}, f32[256,1024]{1,0:T(8,128)}, bf16[256,1024]{1,0:T(8,128)(2,1)}, f32[32]{0:T(128)}, f32[32]{0:T(128)}, /*index=5*/f...) custom-call(bf16[261,16,128]{2,1,0:T(8,128)(2,1)} %bitcast.11, ...), custom_call_target="tpu_custom_call" | custom-call | tf_op jit(solution)/shard_map/finish/pallas_call | solution.py:1548
